TPU v7x, 256 devices: a whole 4x4x8 slice. The times are simulated.
256 devices in a mesh: band: 32 (over x, y, core), grp: 8 (over z).
Axes of the slice: x: 4, y: 4, z: 8, core: 2. Of those that a mesh axis runs over, the one named last changes fastest.
Arguments:
- composition: float32 [1048576, 160], P(('band', 'grp')), may hold values from -3 to 3
- neighbours: int32 [8192, 3], P(('band', 'grp')), may hold values from 0 to 255
- mixing_weights: bfloat16 [8192, 3, 128, 128], P(('band', 'grp')), may hold values from -0.3125 to 0.3125
- slot_order: int32 [256, 4096], P(('band', 'grp')), may hold values from 0 to 4095, each once within a row
- photo_index: int32 [1048576], P(('band', 'grp')), may hold values from 0 to 63
- photo_table: float32 [64, 160], replicated, may hold values from 0.05 to 1
- coupling: float32 [160, 160], replicated, may hold values from -0.5 to 0.5
- loss_rate: float32 [160], replicated, may hold values from 0.05 to 0.5
- preconditioner: float32 [8192, 160, 160], P(('band', 'grp')), may hold values from -0.25 to 1.25
Outputs:
- updated: float32 [1048576, 160], P(('band', 'grp'))
All inputs are finite; a program needn't handle non-finite values.
Results may differ from a plain program's by a relative error of at most 0.0022.
Values may be sent and summed in bfloat16 or wider, within the bound.
No kernel may reach another device: no remote copies, remote signals or barrier semaphores. Data moves between devices by JAX's collectives and lax.ppermute only.
A program may use at most 128 MiB of HBM per device.

v0:
```python
import functools

import jax
import jax.numpy as jnp
from jax import lax
from jax.experimental import pallas as pl
from jax.experimental.pallas import tpu as pltpu
from jax.sharding import PartitionSpec as P

BLOCK = 128
NEWTON = 2
WIDE = 256
LIMIT = 60
GROUPS = 4
LOT = 8
time_step = 0.5

f32 = jnp.float32
bf16 = jnp.bfloat16
VMEM = pl.BlockSpec(memory_space=pltpu.VMEM)
SMEM = pl.BlockSpec(memory_space=pltpu.SMEM)
ANY = pl.BlockSpec(memory_space=pl.ANY)


CHEAP = pl.CostEstimate(flops=1, bytes_accessed=1, transcendentals=0)


def params(mib):
    return pltpu.CompilerParams(vmem_limit_bytes=mib << 20)


def halves(values):
    high = values.astype(bf16)
    return high, (values - high.astype(f32)).astype(bf16)


def pack_kernel(tiles_ref, photo_ref, out_ref):
    count, species, _ = tiles_ref.shape
    rest = species - BLOCK
    fold = BLOCK // rest
    rows = species // fold

    def body(t, _):
        tile = tiles_ref[t].T
        out_ref[t, pl.ds(0, species), :] = tile[:, :BLOCK]
        out_ref[t, pl.ds(species, rows), :] = jnp.concatenate(
            [tile[i * rows : (i + 1) * rows, BLOCK:] for i in range(fold)], axis=1
        )
        entries = photo_ref[pl.ds(t, 1), :].astype(f32)
        out_ref[t, pl.ds(species + rows, 8), :] = jnp.broadcast_to(entries, (8, BLOCK))
        return 0

    lax.fori_loop(0, count, body, 0, unroll=2)


def pack(tiles, photo):
    count, species, _ = tiles.shape
    rows = species + species * (species - BLOCK) // BLOCK + 8
    return pl.pallas_call(
        pack_kernel,
        out_shape=jax.ShapeDtypeStruct((count, rows, BLOCK), f32),
        grid=(count // LOT,),
        in_specs=[
            pl.BlockSpec((LOT, species, species), lambda i: (i, 0, 0)),
            pl.BlockSpec((LOT, BLOCK), lambda i: (i, 0)),
        ],
        out_specs=pl.BlockSpec((LOT, rows, BLOCK), lambda i: (i, 0, 0)),
        compiler_params=params(LIMIT),
        cost_estimate=CHEAP,
    )(tiles, photo)


def unpack_kernel(packed_ref, table_ref, tiles_ref, rates_ref):
    count = packed_ref.shape[0]
    species = rates_ref.shape[0]
    levels = table_ref.shape[1]
    rest = species - BLOCK
    fold = BLOCK // rest
    rows = species // fold
    t_high, t_rest = halves(table_ref[...])
    first = table_ref[...] - t_high.astype(f32)
    t_low = (first - t_rest.astype(f32)).astype(bf16)
    table = jnp.concatenate([t_high, t_rest, t_low], axis=1)

    def body(t, _):
        folded = packed_ref[t, pl.ds(species, rows), :]
        tail = jnp.concatenate(
            [folded[:, i * rest : (i + 1) * rest] for i in range(fold)], axis=0
        )
        tile = jnp.concatenate([packed_ref[t, pl.ds(0, species), :], tail], axis=1)
        high, low = halves(tile)
        tiles_ref[t] = jnp.concatenate([high, low, high], axis=1)
        entries = packed_ref[t, pl.ds(species + rows, 1), :].astype(jnp.int32)
        level = lax.broadcasted_iota(jnp.int32, (levels, BLOCK), 0)
        onehot = (level == entries).astype(f32).astype(bf16)
        onehot = jnp.concatenate([onehot, onehot, onehot], axis=0)
        rates_ref[:, pl.ds(pl.multiple_of(t * BLOCK, BLOCK), BLOCK)] = jnp.dot(
            table, onehot, preferred_element_type=f32
        )
        return 0

    lax.fori_loop(0, count, body, 0, unroll=2)


def unpack(packed, table):
    count = packed.shape[0]
    species = table.shape[0]
    return pl.pallas_call(
        unpack_kernel,
        out_shape=(
            jax.ShapeDtypeStruct((count, species, 3 * species), bf16),
            jax.ShapeDtypeStruct((species, count * BLOCK), f32),
        ),
        grid=(count // LOT,),
        in_specs=[
            pl.BlockSpec((LOT,) + packed.shape[1:], lambda i: (i, 0, 0)),
            pl.BlockSpec(table.shape, lambda i: (0, 0)),
        ],
        out_specs=(
            pl.BlockSpec((LOT, species, 3 * species), lambda i: (i, 0, 0)),
            pl.BlockSpec((species, LOT * BLOCK), lambda i: (0, i)),
        ),
        compiler_params=params(LIMIT),
        cost_estimate=CHEAP,
    )(packed, table)


def select_kernel(slots_ref, out_ref):
    parcels = slots_ref.shape[1]

    def body(t, _):
        off = pl.multiple_of(t * WIDE, WIDE)
        place = slots_ref[:, pl.ds(off, WIDE)] & (WIDE - 1)
        lane = lax.broadcasted_iota(jnp.int32, (WIDE, WIDE), 0)
        out_ref[pl.ds(off, WIDE), :] = (lane == place).astype(f32).T.astype(bf16)
        return 0

    lax.fori_loop(0, parcels // WIDE, body, 0)


def select(slots):
    parcels = slots.shape[1]
    return pl.pallas_call(
        select_kernel,
        out_shape=jax.ShapeDtypeStruct((parcels, WIDE), bf16),
        in_specs=[VMEM],
        out_specs=VMEM,
        compiler_params=params(LIMIT),
        cost_estimate=CHEAP,
    )(slots)


def mix_kernel(first, size, count, *refs):
    codes_ref, slots_ref, weights_ref, comp_ref, select_ref = refs[:5]
    parts = refs[5 : 5 + count]
    mixed_ref, start_ref, held, own, weights, chosen, both, stack, sems = refs[5 + count :]
    parcels = mixed_ref.shape[1]
    blocks = parcels // BLOCK
    wide = parcels // WIDE
    half = size // 32 * 16
    lots = 4
    lot = blocks // lots
    copies = []
    for place in range(7):
        spot = place if place < 4 else place + 1
        copies.append((parts[place], held.at[spot]))
    copies.append((parts[7], held.at[4, pl.ds(0, half), :]))
    copies.append((parts[8], held.at[4, pl.ds(half, size - half), :]))
    copies.append((comp_ref.at[pl.ds(first, size), :], own))
    early = len(copies)
    for n in range(lots):
        copies.append((weights_ref.at[pl.ds(n * lot, lot)], weights.at[pl.ds(n * lot, lot)]))
    copies.append((select_ref, chosen))
    copies = [
        pltpu.make_async_copy(source, target, sems.at[i])
        for i, (source, target) in enumerate(copies)
    ]
    for copy in copies:
        copy.start()
    for copy in copies[:early]:
        copy.wait()

    def mix(c, _):
        picked = []
        for k in range(weights.shape[1]):
            code = codes_ref[c, k]
            column = pl.multiple_of((code & (blocks - 1)) * BLOCK, BLOCK)
            picked.append(held[lax.div(code, blocks), :, pl.ds(column, BLOCK)])
        rows = jnp.concatenate(picked, axis=1)
        block = jnp.concatenate([weights[c, k] for k in range(weights.shape[1])], axis=1)
        term = lax.dot_general(
            rows, block, (((1,), (1,)), ((), ())), preferred_element_type=f32
        )
        off = pl.multiple_of(c * BLOCK, BLOCK)
        mixed_ref[:, pl.ds(off, BLOCK)] = own[:, pl.ds(off, BLOCK)] + term
        return 0

    for n in range(lots):
        copies[early + n].wait()
        lax.fori_loop(n * lot, (n + 1) * lot, mix, 0, unroll=lot)
    high, low = halves(mixed_ref[...])
    both[pl.ds(0, size), :] = high
    both[pl.ds(size, size), :] = low
    copies[early + lots].wait()

    def move(i, _):
        group = slots_ref[...] >> 8
        for j in range(GROUPS):
            keep = (group == i * GROUPS + j).astype(f32).astype(bf16)
            stack[pl.ds(j * 2 * size, 2 * size), :] = both[...] * keep
        moved = jnp.dot(stack[...], chosen[...], preferred_element_type=f32)
        for j in range(GROUPS):
            at = j * 2 * size
            off = pl.multiple_of((i * GROUPS + j) * WIDE, WIDE)
            start_ref[:, pl.ds(off, WIDE)] = (
                moved[at : at + size] + moved[at + size : at + 2 * size]
            )
        return 0

    lax.fori_loop(0, wide // GROUPS, move, 0)


def mix(first, size, codes, weights, comp, slots, chosen, parts):
    parcels = comp.shape[1]
    shape = jax.ShapeDtypeStruct((size, parcels), f32)
    return pl.pallas_call(
        functools.partial(mix_kernel, first, size, len(parts)),
        out_shape=(shape, shape),
        in_specs=[SMEM, VMEM] + [ANY] * (3 + len(parts)),
        out_specs=(VMEM, VMEM),
        scratch_shapes=[
            pltpu.VMEM((8, size, parcels), bf16),
            pltpu.VMEM((size, parcels), f32),
            pltpu.VMEM(weights.shape, bf16),
            pltpu.VMEM(chosen.shape, bf16),
            pltpu.VMEM((2 * size, parcels), bf16),
            pltpu.VMEM((GROUPS * 2 * size, parcels), bf16),
            pltpu.SemaphoreType.DMA((15,)),
        ],
        compiler_params=params(LIMIT),
        cost_estimate=CHEAP,
    )(codes, slots, weights, comp, chosen, *parts)


BATCH = 4


def finish_kernel(
    near_ref, slots_ref, yields_ref, loss_ref,
    gathered_ref, weights_ref, comp_ref, select_ref, mixed_ref, start_ref, rates_ref, tiles_ref,
    out_ref,
    held, weights, chosen, home, both, stack, begun, rates_in, tiles, delta, result,
    sems, lot_sems, out_sems,
):
    species, parcels = rates_in.shape
    size = held.shape[1]
    blocks = parcels // BLOCK
    wide = parcels // WIDE
    span = BATCH * BLOCK
    batches = parcels // span
    lots = 4
    lot = blocks // lots
    rest = species - size
    first_copies = [
        pltpu.make_async_copy(gathered_ref, held, sems.at[0]),
        pltpu.make_async_copy(
            comp_ref.at[pl.ds(0, size), :], home.at[pl.ds(0, size), :], sems.at[1]
        ),
    ]
    weight_copies = [
        pltpu.make_async_copy(
            weights_ref.at[pl.ds(n * lot, lot)], weights.at[pl.ds(n * lot, lot)], sems.at[2 + n]
        )
        for n in range(lots)
    ]
    select_copy = pltpu.make_async_copy(select_ref, chosen, sems.at[2 + lots])
    home_copy = pltpu.make_async_copy(
        mixed_ref, home.at[pl.ds(size, rest), :], sems.at[3 + lots]
    )
    start_copy = pltpu.make_async_copy(
        start_ref, begun.at[pl.ds(size, rest), :], sems.at[4 + lots]
    )
    lot_copies = []
    for b in range(batches):
        column = pl.ds(b * span, span)
        lot_copies.append(
            pltpu.make_async_copy(
                rates_ref.at[:, column], rates_in.at[:, column], lot_sems.at[b, 0]
            )
        )
        lot_copies.append(
            pltpu.make_async_copy(
                tiles_ref.at[pl.ds(b * BATCH, BATCH)],
                tiles.at[pl.ds(b * BATCH, BATCH)],
                lot_sems.at[b, 1],
            )
        )
    for copy in (
        first_copies + weight_copies + [select_copy, start_copy] + lot_copies + [home_copy]
    ):
        copy.start()
    for copy in first_copies:
        copy.wait()

    def mix(c, _):
        picked = []
        for k in range(weights.shape[1]):
            block = near_ref[c, k]
            column = pl.multiple_of((block & (blocks - 1)) * BLOCK, BLOCK)
            picked.append(held[lax.div(block, blocks), :, pl.ds(column, BLOCK)])
        rows = jnp.concatenate(picked, axis=1)
        block = jnp.concatenate([weights[c, k] for k in range(weights.shape[1])], axis=1)
        term = lax.dot_general(
            rows, block, (((1,), (1,)), ((), ())), preferred_element_type=f32
        )
        off = pl.multiple_of(c * BLOCK, BLOCK)
        total = home[pl.ds(0, size), pl.ds(off, BLOCK)] + term
        home[pl.ds(0, size), pl.ds(off, BLOCK)] = total
        high, low = halves(total)
        both[pl.ds(0, size), pl.ds(off, BLOCK)] = high
        both[pl.ds(size, size), pl.ds(off, BLOCK)] = low
        return 0

    for n in range(lots):
        weight_copies[n].wait()
        lax.fori_loop(n * lot, (n + 1) * lot, mix, 0, unroll=lot)
    select_copy.wait()

    def move(i, _):
        group = slots_ref[...] >> 8
        for j in range(GROUPS):
            keep = (group == i * GROUPS + j).astype(f32).astype(bf16)
            stack[pl.ds(j * 2 * size, 2 * size), :] = both[...] * keep
        moved = jnp.dot(stack[...], chosen[...], preferred_element_type=f32)
        for j in range(GROUPS):
            at = j * 2 * size
            off = pl.multiple_of((i * GROUPS + j) * WIDE, WIDE)
            begun[pl.ds(0, size), pl.ds(off, WIDE)] = (
                moved[at : at + size] + moved[at + size : at + 2 * size]
            )
        return 0

    lax.fori_loop(0, wide // GROUPS, move, 0)
    start_copy.wait()
    y_high, y_low = halves(yields_ref[...])
    yields = jnp.concatenate([y_high, y_low, y_high], axis=1)
    loss = loss_ref[...]

    def spread(values):
        high, low = halves(values)
        return jnp.concatenate([high, high, low], axis=0)

    for b in range(batches):
        lot_copies[2 * b].wait()
        lot_copies[2 * b + 1].wait()
        off = b * span
        start = begun[:, pl.ds(off, span)]
        rates = rates_in[:, pl.ds(off, span)]
        current = start
        for newton_step in range(NEWTON):
            forcing = (
                jnp.dot(yields, spread(current * rates), preferred_element_type=f32)
                - loss * current * current
            )
            defect = current - start - time_step * forcing
            wings = spread(defect)
            update = [
                jnp.dot(
                    tiles[b * BATCH + i],
                    wings[:, i * BLOCK : (i + 1) * BLOCK],
                    preferred_element_type=f32,
                )
                for i in range(BATCH)
            ]
            current = current - jnp.concatenate(update, axis=1)
        change = (current - start).astype(bf16)
        for i in range(span // WIDE):
            delta[pl.ds((b * span // WIDE + i) * species, species), :] = change[
                :, i * WIDE : (i + 1) * WIDE
            ]

    home_copy.wait()
    outs = []
    for t in range(wide):
        off = t * WIDE
        slots = slots_ref[:, pl.ds(off, WIDE)]
        lane = lax.broadcasted_iota(jnp.int32, (WIDE, WIDE), 0)
        picks = (lane == (slots & (WIDE - 1))).astype(f32).astype(bf16)
        group = slots >> 8
        total = jnp.zeros((species, WIDE), f32)
        for j in range(wide):
            moved = jnp.dot(
                delta[pl.ds(j * species, species), :], picks, preferred_element_type=f32
            )
            total = jnp.where(group == j, moved, total)
        result[:, pl.ds(off, WIDE)] = home[:, pl.ds(off, WIDE)] + total
        out = pltpu.make_async_copy(
            result.at[:, pl.ds(off, WIDE)], out_ref.at[:, pl.ds(off, WIDE)], out_sems.at[t]
        )
        out.start()
        outs.append(out)
    for out in outs:
        out.wait()


def finish(neighbours, slots, yields, loss, gathered, weights, comp, chosen, mixed, start, rates, tiles):
    species, parcels = rates.shape
    size = gathered.shape[1]
    batches = parcels // (BATCH * BLOCK)
    whole = pltpu.VMEM((species, parcels), f32)
    return pl.pallas_call(
        finish_kernel,
        out_shape=jax.ShapeDtypeStruct((species, parcels), f32),
        in_specs=[SMEM] + [VMEM] * 3 + [ANY] * 8,
        out_specs=ANY,
        scratch_shapes=[
            pltpu.VMEM(gathered.shape, bf16),
            pltpu.VMEM(weights.shape, bf16),
            pltpu.VMEM(chosen.shape, bf16),
            whole,
            pltpu.VMEM((2 * size, parcels), bf16),
            pltpu.VMEM((GROUPS * 2 * size, parcels), bf16),
            whole,
            whole,
            pltpu.VMEM(tiles.shape, bf16),
            pltpu.VMEM((parcels // WIDE * species, WIDE), bf16),
            whole,
            pltpu.SemaphoreType.DMA((9,)),
            pltpu.SemaphoreType.DMA((batches, 2)),
            pltpu.SemaphoreType.DMA((parcels // WIDE,)),
        ],
        compiler_params=params(LIMIT),
        cost_estimate=CHEAP,
    )(neighbours, slots, yields, loss, gathered, weights, comp, chosen, mixed, start, rates, tiles)


def after(values, gates):
    both = lax.optimization_barrier(tuple(values) + tuple(gates))
    return both[: len(values)], both[len(values) :]


def hop(sides):
    size = lax.axis_size("grp")
    right = [(i, (i + 1) % size) for i in range(size)]
    left = [(i, (i - 1) % size) for i in range(size)]
    return lax.ppermute(sides[0], "grp", right), lax.ppermute(sides[1], "grp", left)


def rows(sides, first, size):
    return tuple(side[first : first + size] for side in sides)


def halves_of(sides):
    half = sides[0].shape[0] // 32 * 16
    return sides[0][:half], sides[1][half:]


SIZES = (112, 48)


def shards(
    composition,
    neighbours,
    mixing_weights,
    slot_order,
    photo_index,
    photo_table,
    coupling,
    loss_rate,
    preconditioner,
):
    parcels, species = composition.shape
    blocks = parcels // BLOCK
    ring_size = lax.axis_size("grp")
    comp = composition.T
    firsts = [sum(SIZES[:i]) for i in range(len(SIZES))]
    place = neighbours // blocks
    distance = (lax.axis_index("grp") - place) % ring_size
    codes = distance * blocks + neighbours % blocks

    pieces = [comp[first : first + size] for first, size in zip(firsts, SIZES)]
    a_own = pieces[0].astype(bf16)
    (b_piece,), (a_own,) = after(pieces[1:], (a_own,))
    b_own = b_piece.astype(bf16)
    gathered = lax.all_gather(a_own, "grp", axis=0)
    b_one = hop((b_own, b_own))
    (tiles_in, photo_in), b_one = after(
        (preconditioner, photo_index.reshape(blocks, BLOCK)), b_one
    )
    packed = pack(tiles_in, photo_in)
    arrived = lax.all_to_all(packed, "band", split_axis=0, concat_axis=0, tiled=True)
    b_two = hop(b_one)
    chosen = select(slot_order)
    b_two, (chosen,) = after(b_two, (chosen,))
    b_three = hop(b_two)
    (arrived,), b_three = after((arrived,), b_three)
    tiles, rates = unpack(arrived, photo_table.T)
    b_four = hop(halves_of(b_three))
    parts = [b_own, b_one[0], b_two[0], b_three[0], b_three[1], b_two[1], b_one[1], *b_four]
    mixed_b = mix(
        firsts[1], SIZES[1], codes, mixing_weights, comp, slot_order, chosen, parts
    )
    (gathered,), gates = after((gathered,), (tiles, rates, *mixed_b))
    tiles, rates, *mixed_b = gates
    updated = finish(
        neighbours, slot_order, coupling.T, loss_rate.reshape(species, 1),
        gathered, mixing_weights, comp, chosen, *mixed_b, rates, tiles,
    )
    return updated.T


def solution(mesh):
    placed = (
        P(("band", "grp"), None),
        P(("band", "grp"), None),
        P(("band", "grp"), None, None, None),
        P(("band", "grp"), None),
        P(("band", "grp")),
        P(),
        P(),
        P(),
        P(("band", "grp"), None, None),
    )
    return jax.shard_map(
        shards, mesh=mesh, in_specs=placed, out_specs=P(("band", "grp"), None), check_vma=False
    )
```

profile of v0, /device:TPU:1, one launch (start us, length us, event | category | flops | bytes accessed | tf_op | source)
XLA Modules:
  0.0 157.9 jit_solution(13689967912719274917)
XLA Ops:
  6.5 2.5 %slice.20 = bf16[112,4096]{1,0:T(8,128)(2,1)} slice(f32[160,4096]{1,0:T(8,128)} %bitcast.7), slice={[0:112], [0:4096]} | slice | bytes 1835008 | tf_op jit(solution)/shard_map/slice | solution.py:481
  9.1 1.2 slice.17.refs_5_
  10.3 2.5 %collective-permute-start = (bf16[48,4096]{1,0:T(8,128)(2,1)S(1)}, bf16[48,4096]{1,0:T(8,128)(2,1)S(1)}, u32[]{:S(2)}, u32[]{:S(2)}) collective-permute-start(bf16[48,4096]{1,0:T(8,128)(2,1)S(1)} %slice.17.refs_5_), channel_id=1, source_target_pairs={{0,1},{1,2},{2,3},{3,4},{4,5},{5,6},{6,7},{7,0},{8,9},{9,10},{10,1... | collective-permute-start | bytes 1179656 | tf_op jit(solution)/shard_map/ppermute | solution.py:446
  12.8 4.0 %collective-permute-start.1 = (bf16[48,4096]{1,0:T(8,128)(2,1)S(1)}, bf16[48,4096]{1,0:T(8,128)(2,1)S(1)}, u32[]{:S(2)}, u32[]{:S(2)}) collective-permute-start(bf16[48,4096]{1,0:T(8,128)(2,1)S(1)} %slice.17.refs_5_), channel_id=1, source_target_pairs={{0,7},{1,0},{2,1},{3,2},{4,3},{5,4},{6,5},{7,6},{8,15},{9,8},{10,9... | collective-permute-start | bytes 1179656 | tf_op jit(solution)/shard_map/ppermute | solution.py:446
  16.8 8.8 %collective-permute-done.refs_6_ = bf16[48,4096]{1,0:T(8,128)(2,1)S(1)} collective-permute-done((bf16[48,4096]{1,0:T(8,128)(2,1)S(1)}, bf16[48,4096]{1,0:T(8,128)(2,1)S(1)}, u32[]{:S(2)}, u32[]{:S(2)}) %collective-permute-start) | collective-permute-done | bytes 393248 | tf_op jit(solution)/shard_map/ppermute | solution.py:446
  26.4 0.8 copy-done.4
  27.1 7.0 %shard_map.91 = f32[32,208,128]{2,1,0:T(8,128)} custom-call(f32[32,160,160]{2,1,0:T(8,128)} %tiles_ref, s32[32,128]{1,0:T(8,128)} %bitcast.14), custom_call_target="tpu_custom_call" | custom-call | flops 1 | bytes 1 | tf_op jit(solution)/shard_map/pallas_call | solution.py:59
  34.1 8.5 %all-to-all-start = ((f32[32,208,128]{2,1,0:T(8,128)}), f32[32,208,128]{2,1,0:T(8,128)S(1)}, u32[]{:S(2)}, u32[]{:S(2)}) async-start(f32[32,208,128]{2,1,0:T(8,128)} %shard_map.91), calls=%async_computation | async-start | bytes 6815744 | tf_op jit(solution)/shard_map/all_to_all | solution.py:491
  42.7 2.7 %collective-permute-start.3 = (bf16[48,4096]{1,0:T(8,128)(2,1)}, bf16[48,4096]{1,0:T(8,128)(2,1)}, u32[]{:S(2)}, u32[]{:S(2)}) collective-permute-start(bf16[48,4096]{1,0:T(8,128)(2,1)} %copy-done.4), channel_id=1, source_target_pairs={{0,7},{1,0},{2,1},{3,2},{4,3},{5,4},{6,5},{7,6},{8,15},{9,8},{10,9... | collective-permute-start | bytes 1179656 | tf_op jit(solution)/shard_map/ppermute | solution.py:446
  45.4 3.8 %shard_map.92.refs_4_.select_ref = bf16[4096,256]{1,0:T(8,128)(2,1)} custom-call(s32[1,4096]{1,0:T(1,128)} %slots_ref.3), custom_call_target="tpu_custom_call" | custom-call | flops 1 | bytes 1 | tf_op jit(solution)/shard_map/pallas_call | solution.py:143
  49.2 14.3 %collective-permute-done.2.refs_7_ = bf16[48,4096]{1,0:T(8,128)(2,1)S(1)} collective-permute-done((bf16[48,4096]{1,0:T(8,128)(2,1)}, bf16[48,4096]{1,0:T(8,128)(2,1)S(1)}, u32[]{:S(2)}, u32[]{:S(2)}) %collective-permute-start.2) | collective-permute-done | bytes 393248 | tf_op jit(solution)/shard_map/ppermute | solution.py:446
  63.5 1.4 collective-permute-start.4
  64.9 1.2 collective-permute-start.5
  66.2 17.7 %collective-permute-done.4.refs_8_ = bf16[48,4096]{1,0:T(8,128)(2,1)S(1)} collective-permute-done((bf16[48,4096]{1,0:T(8,128)(2,1)S(1)}, bf16[48,4096]{1,0:T(8,128)(2,1)S(1)}, u32[]{:S(2)}, u32[]{:S(2)}) %collective-permute-start.4) | collective-permute-done | bytes 393248 | tf_op jit(solution)/shard_map/ppermute | solution.py:446
  83.9 0.8 copy-done.2
  85.2 1.8 %slice.16 = bf16[32,4096]{1,0:T(8,128)(2,1)} slice(bf16[48,4096]{1,0:T(8,128)(2,1)} %collective-permute-done.5.refs_9_), slice={[16:48], [0:4096]} | slice | bytes 524288 | tf_op jit(solution)/shard_map/slice | solution.py:455
  87.1 2.7 %collective-permute-start.7 = (bf16[32,4096]{1,0:T(8,128)(2,1)}, bf16[32,4096]{1,0:T(8,128)(2,1)}, u32[]{:S(2)}, u32[]{:S(2)}) collective-permute-start(bf16[32,4096]{1,0:T(8,128)(2,1)} %slice.16), channel_id=1, source_target_pairs={{0,7},{1,0},{2,1},{3,2},{4,3},{5,4},{6,5},{7,6},{8,15},{9,8},{10,9... | collective-permute-start | bytes 786440 | tf_op jit(solution)/shard_map/ppermute | solution.py:446
  90.5 1.7 %copy.17 = f32[160,160]{0,1:T(8,128)} copy(f32[160,160]{1,0:T(8,128)} %param.15) | data formatting | bytes 204800 | tf_op args[6]
  93.0 0.9 slice.15
  94.8 7.6 %shard_map.93 = (bf16[32,160,480]{2,1,0:T(8,128)(2,1)}, f32[160,4096]{1,0:T(8,128)}) custom-call(f32[32,208,128]{2,1,0:T(8,128)} %copy-done, f32[160,64]{1,0:T(8,128)} %bitcast.13), custom_call_target="tpu_custom_call" | custom-call | flops 1 | bytes 1 | tf_op jit(solution)/shard_map/pallas_call | solution.py:108
  102.4 0.8 collective-permute-done.6.refs_12_
  103.8 10.3 %shard_map.94 = (f32[48,4096]{1,0:T(8,128)}, f32[48,4096]{1,0:T(8,128)}) custom-call(s32[32,3]{1,0:T(8,128)} %fusion.3.refs_0_, s32[1,4096]{1,0:T(1,128)} %slots_ref.3, bf16[32,3,128,128]{3,2,1,0:T(8,128)(2,1)} %weights_ref.1, f32[160,4096]{1,0:T(8,128)} %bitcast.9, bf16[4096,256]{1,0:T(8,128)(2,1)} %shard_map.92.refs_4_.select_ref, ...), custom_call_target="tpu_custom_call" | custom-call | flops 1 | bytes 1 | tf_op jit(solution)/shard_map/pallas_call | solution.py:226
  114.2 5.0 %all-gather.3.cloned.1.call-done = bf16[896,4096]{1,0:T(8,128)(2,1)} async-done(((bf16[112,4096]{1,0:T(8,128)(2,1)}), bf16[896,4096]{1,0:T(8,128)(2,1)}) %all-gather.3.cloned.1.call-update) | async-done | bytes 7340048 | tf_op jit(solution)/shard_map/all_gather | solution.py:485
  119.2 31.9 %shard_map.95 = f32[160,4096]{1,0:T(8,128)} custom-call(s32[32,3]{1,0:T(8,128)} %copy-done.6, s32[1,4096]{1,0:T(1,128)} %slots_ref.3, f32[160,160]{1,0:T(8,128)} %bitcast.12, f32[160,1]{1,0:T(8,128)} %copy.24.loss_ref, bf16[8,112,4096]{2,1,0:T(8,128)(2,1)} %bitcast.11, bf16[32,3,128,128]{3,2,1,0:T(8,128)(2,1)} %weights_ref.1, f32[160,4096]{1,0:T(8,128)} %bitcast.10, ...), custom_call_target="tpu_custom_call" | custom-call | flops 1 | bytes 1 | tf_op jit(solution)/shard_map/pallas_call | solution.py:411
  (33 shorter events, 4.6 us)
Async XLA Ops:
  6.5 112.7 %all-gather.3.cloned.1.call-start = ((), (), s32[]{:S(2)}) async-start(), calls=%async_computation.1 | async-start | bytes 8257536 | tf_op jit(solution)/shard_map/all_gather | solution.py:485
  10.2 23.8 %copy-start.1 = (bf16[48,4096]{1,0:T(8,128)(2,1)}, bf16[48,4096]{1,0:T(8,128)(2,1)S(1)}, u32[]{:S(2)}) copy-start(bf16[48,4096]{1,0:T(8,128)(2,1)S(1)} %slice.17.refs_5_) | copy-start | bytes 1179652
  10.3 15.3 %collective-permute-start = (bf16[48,4096]{1,0:T(8,128)(2,1)S(1)}, bf16[48,4096]{1,0:T(8,128)(2,1)S(1)}, u32[]{:S(2)}, u32[]{:S(2)}) collective-permute-start(bf16[48,4096]{1,0:T(8,128)(2,1)S(1)} %slice.17.refs_5_), channel_id=1, source_target_pairs={{0,1},{1,2},{2,3},{3,4},{4,5},{5,6},{6,7},{7,0},{8,9},{9,10},{10,1... | collective-permute-start | bytes 1179656 | tf_op jit(solution)/shard_map/ppermute | solution.py:446
  12.8 12.8 %collective-permute-start.1 = (bf16[48,4096]{1,0:T(8,128)(2,1)S(1)}, bf16[48,4096]{1,0:T(8,128)(2,1)S(1)}, u32[]{:S(2)}, u32[]{:S(2)}) collective-permute-start(bf16[48,4096]{1,0:T(8,128)(2,1)S(1)} %slice.17.refs_5_), channel_id=1, source_target_pairs={{0,7},{1,0},{2,1},{3,2},{4,3},{5,4},{6,5},{7,6},{8,15},{9,8},{10,9... | collective-permute-start | bytes 1179656 | tf_op jit(solution)/shard_map/ppermute | solution.py:446
  25.6 0.8 copy-start.3
  26.4 0.8 copy-start.4
  34.1 55.6 %copy-start.9 = (s32[32,3]{0,1:T(4,128)S(1)}, s32[32,3]{0,1:T(4,128)}, u32[]{:S(2)}) copy-start(s32[32,3]{0,1:T(4,128)} %param.10) | copy-start | bytes 1156
  34.1 55.7 %copy-start.8 = (f32[64,160]{1,0:T(8,128)S(1)}, f32[64,160]{1,0:T(8,128)}, u32[]{:S(2)}) copy-start(f32[64,160]{1,0:T(8,128)} %param.14) | copy-start | bytes 122884
  34.1 58.1 %copy-start.10 = (f32[160]{0:T(256)S(1)}, f32[160]{0:T(256)}, u32[]{:S(2)}) copy-start(f32[160]{0:T(256)} %param.16) | copy-start | bytes 1924
  34.1 51.1 %all-to-all-start = ((f32[32,208,128]{2,1,0:T(8,128)}), f32[32,208,128]{2,1,0:T(8,128)S(1)}, u32[]{:S(2)}, u32[]{:S(2)}) async-start(f32[32,208,128]{2,1,0:T(8,128)} %shard_map.91), calls=%async_computation | async-start | bytes 6815744 | tf_op jit(solution)/shard_map/all_to_all | solution.py:491
  42.6 20.9 %collective-permute-start.2 = (bf16[48,4096]{1,0:T(8,128)(2,1)}, bf16[48,4096]{1,0:T(8,128)(2,1)S(1)}, u32[]{:S(2)}, u32[]{:S(2)}) collective-permute-start(bf16[48,4096]{1,0:T(8,128)(2,1)} %copy-done.3), channel_id=1, source_target_pairs={{0,1},{1,2},{2,3},{3,4},{4,5},{5,6},{6,7},{7,0},{8,9},{9,10},{10,1... | collective-permute-start | bytes 1179656 | tf_op jit(solution)/shard_map/ppermute | solution.py:446
  42.7 20.8 %collective-permute-start.3 = (bf16[48,4096]{1,0:T(8,128)(2,1)}, bf16[48,4096]{1,0:T(8,128)(2,1)}, u32[]{:S(2)}, u32[]{:S(2)}) collective-permute-start(bf16[48,4096]{1,0:T(8,128)(2,1)} %copy-done.4), channel_id=1, source_target_pairs={{0,7},{1,0},{2,1},{3,2},{4,3},{5,4},{6,5},{7,6},{8,15},{9,8},{10,9... | collective-permute-start | bytes 1179656 | tf_op jit(solution)/shard_map/ppermute | solution.py:446
  63.5 20.4 %copy-start.5 = (bf16[48,4096]{1,0:T(8,128)(2,1)}, bf16[48,4096]{1,0:T(8,128)(2,1)S(1)}, u32[]{:S(2)}) copy-start(bf16[48,4096]{1,0:T(8,128)(2,1)S(1)} %collective-permute-done.2.refs_7_) | copy-start | bytes 1179652
  63.5 20.4 %collective-permute-start.4 = (bf16[48,4096]{1,0:T(8,128)(2,1)S(1)}, bf16[48,4096]{1,0:T(8,128)(2,1)S(1)}, u32[]{:S(2)}, u32[]{:S(2)}) collective-permute-start(bf16[48,4096]{1,0:T(8,128)(2,1)S(1)} %collective-permute-done.2.refs_7_), channel_id=1, source_target_pairs={{0,1},{1,2},{2,3},{3,4},{4,5},{5,6},{6,7},{7,0},{8,9},{9,10},{10,1... | collective-permute-start | bytes 1179656 | tf_op jit(solution)/shard_map/ppermute | solution.py:446
  64.9 19.7 %collective-permute-start.5 = (bf16[48,4096]{1,0:T(8,128)(2,1)}, bf16[48,4096]{1,0:T(8,128)(2,1)}, u32[]{:S(2)}, u32[]{:S(2)}) collective-permute-start(bf16[48,4096]{1,0:T(8,128)(2,1)} %collective-permute-done.3.refs_10_), channel_id=1, source_target_pairs={{0,7},{1,0},{2,1},{3,2},{4,3},{5,4},{6,5},{7,6},{8,15},{9,8},{10,9... | collective-permute-start | bytes 1179656 | tf_op jit(solution)/shard_map/ppermute | solution.py:446
  83.9 0.8 copy-start.2
  85.2 9.6 %copy-start = (f32[32,208,128]{2,1,0:T(8,128)}, f32[32,208,128]{2,1,0:T(8,128)S(1)}, u32[]{:S(2)}) copy-start(f32[32,208,128]{2,1,0:T(8,128)S(1)} %all-to-all-done.packed_ref) | copy-start | bytes 10223620
  87.1 16.2 %collective-permute-start.7 = (bf16[32,4096]{1,0:T(8,128)(2,1)}, bf16[32,4096]{1,0:T(8,128)(2,1)}, u32[]{:S(2)}, u32[]{:S(2)}) collective-permute-start(bf16[32,4096]{1,0:T(8,128)(2,1)} %slice.16), channel_id=1, source_target_pairs={{0,7},{1,0},{2,1},{3,2},{4,3},{5,4},{6,5},{7,6},{8,15},{9,8},{10,9... | collective-permute-start | bytes 786440 | tf_op jit(solution)/shard_map/ppermute | solution.py:446
  89.8 24.3 %copy-start.6 = (s32[32,3]{1,0:T(8,128)}, s32[32,3]{1,0:T(8,128)S(1)}, u32[]{:S(2)}) copy-start(s32[32,3]{1,0:T(8,128)S(1)} %copy.23.near_ref) | copy-start | bytes 1156
  93.9 9.3 %collective-permute-start.6 = (bf16[16,4096]{1,0:T(8,128)(2,1)S(1)}, bf16[16,4096]{1,0:T(8,128)(2,1)S(1)}, u32[]{:S(2)}, u32[]{:S(2)}) collective-permute-start(bf16[16,4096]{1,0:T(8,128)(2,1)S(1)} %slice.15), channel_id=1, source_target_pairs={{0,1},{1,2},{2,3},{3,4},{4,5},{5,6},{6,7},{7,0},{8,9},{9,10},{10,1... | collective-permute-start | bytes 393224 | tf_op jit(solution)/shard_map/ppermute | solution.py:446
  103.2 0.6 copy-start.7
Sparse Core Ops, SparseCore 0:
  10.4 108.7 all-gather.2
where the time goes:
time: 159 us; the launch traced here: 158 us
  Pallas kernels  60.5 us (38%)
  waiting for transfers between devices  47.2 us (30%)
  starting transfers between devices  23.5 us (15%)
  between operations  13.5 us (8%)
  local copies, waits for them, and re-layouts  12.6 us (8%)
    ppermute x4, waiting for transfers between devices, hop(): lax.ppermute(sides[0], 'grp', right)  41.6 us
    pallas_call x1, Pallas kernels, finish(): pl.pallas_call(finish_kernel, out_shape=jax.ShapeDtypeStruct((species, pa...  31.9 us
    ppermute x4, starting transfers between devices, hop(): lax.ppermute(sides[1], 'grp', left)  10.7 us
    pallas_call x1, Pallas kernels, mix(): pl.pallas_call(functools.partial(mix_kernel, first, size, len(parts)), ou...  10.3 us
    all_to_all x1, starting transfers between devices, shards(): lax.all_to_all(packed, 'band', split_axis=0, concat_axis=0, tiled=True)  8.46 us
    pallas_call x1, Pallas kernels, unpack(): pl.pallas_call(unpack_kernel, out_shape=(jax.ShapeDtypeStruct((count, spe...  7.59 us
    pallas_call x1, Pallas kernels, pack(): pl.pallas_call(pack_kernel, out_shape=jax.ShapeDtypeStruct((count, rows,...  6.97 us
    unnamed x25, local copies, waits for them, and re-layouts  5.43 us
  transfers between devices with their start and end apart: 10, of which 6 were waited for; matrix products, arithmetic and copies ran while one was open for 4% of the time, Pallas kernels for 18%

commit v1 on v0

--- a/solution.py
+++ b/solution.py
@@ -11,7 +11,7 @@
 NEWTON = 2
 WIDE = 256
 LIMIT = 60
-GROUPS = 4
+GROUPS = 2
 LOT = 8
 time_step = 0.5
 
@@ -41,7 +41,7 @@
     rows = species // fold
 
     def body(t, _):
-        tile = tiles_ref[t].T
+        tile = tiles_ref[t]
         out_ref[t, pl.ds(0, species), :] = tile[:, :BLOCK]
         out_ref[t, pl.ds(species, rows), :] = jnp.concatenate(
             [tile[i * rows : (i + 1) * rows, BLOCK:] for i in range(fold)], axis=1
@@ -88,7 +88,7 @@
             [folded[:, i * rest : (i + 1) * rest] for i in range(fold)], axis=0
         )
         tile = jnp.concatenate([packed_ref[t, pl.ds(0, species), :], tail], axis=1)
-        high, low = halves(tile)
+        high, low = halves(tile.T)
         tiles_ref[t] = jnp.concatenate([high, low, high], axis=1)
         entries = packed_ref[t, pl.ds(species + rows, 1), :].astype(jnp.int32)
         level = lax.broadcasted_iota(jnp.int32, (levels, BLOCK), 0)
@@ -242,7 +242,7 @@
     )(codes, slots, weights, comp, chosen, *parts)
 
 
-BATCH = 4
+BATCH = 16
 
 
 def finish_kernel(
@@ -326,22 +326,29 @@
         lax.fori_loop(n * lot, (n + 1) * lot, mix, 0, unroll=lot)
     select_copy.wait()
 
-    def move(i, _):
-        group = slots_ref[...] >> 8
+    group = slots_ref[...] >> 8
+
+    def lay(i):
         for j in range(GROUPS):
             keep = (group == i * GROUPS + j).astype(f32).astype(bf16)
-            stack[pl.ds(j * 2 * size, 2 * size), :] = both[...] * keep
-        moved = jnp.dot(stack[...], chosen[...], preferred_element_type=f32)
+            stack[i % 2, pl.ds(j * 2 * size, 2 * size), :] = both[...] * keep
+
+    lay(0)
+    for i in range(wide // GROUPS):
+        if i + 1 < wide // GROUPS:
+            lay(i + 1)
+        moved = jnp.dot(stack[i % 2], chosen[...], preferred_element_type=f32)
         for j in range(GROUPS):
             at = j * 2 * size
-            off = pl.multiple_of((i * GROUPS + j) * WIDE, WIDE)
+            off = (i * GROUPS + j) * WIDE
             begun[pl.ds(0, size), pl.ds(off, WIDE)] = (
                 moved[at : at + size] + moved[at + size : at + 2 * size]
             )
-        return 0
-
-    lax.fori_loop(0, wide // GROUPS, move, 0)
+
     start_copy.wait()
+    home_copy.wait()
+    for copy in lot_copies:
+        copy.wait()
     y_high, y_low = halves(yields_ref[...])
     yields = jnp.concatenate([y_high, y_low, y_high], axis=1)
     loss = loss_ref[...]
@@ -351,8 +358,6 @@
         return jnp.concatenate([high, high, low], axis=0)
 
     for b in range(batches):
-        lot_copies[2 * b].wait()
-        lot_copies[2 * b + 1].wait()
         off = b * span
         start = begun[:, pl.ds(off, span)]
         rates = rates_in[:, pl.ds(off, span)]
@@ -379,7 +384,6 @@
                 :, i * WIDE : (i + 1) * WIDE
             ]
 
-    home_copy.wait()
     outs = []
     for t in range(wide):
         off = t * WIDE
@@ -419,7 +423,7 @@
             pltpu.VMEM(chosen.shape, bf16),
             whole,
             pltpu.VMEM((2 * size, parcels), bf16),
-            pltpu.VMEM((GROUPS * 2 * size, parcels), bf16),
+            pltpu.VMEM((2, GROUPS * 2 * size, parcels), bf16),
             whole,
             whole,
             pltpu.VMEM(tiles.shape, bf16),

time: 159 us -> 153 us (0.962)
  Pallas kernels: 60.5 us -> 56.5 us
  waiting for transfers between devices: 47.2 us -> 45.5 us
    pallas_call x1, Pallas kernels: 31.9 us -> 26.1 us  [finish(): pl.pallas_call(finish_kernel, out_shape=jax.ShapeDtypeStruct((species, pa...]
    pallas_call x1, Pallas kernels: 7.59 us -> 10 us  [unpack(): pl.pallas_call(unpack_kernel, out_shape=(jax.ShapeDtypeStruct((count, spe...]
  transfers between devices with their start and end apart: 10 -> 10, of which waited for: 6 -> 5; matrix products, arithmetic and copies ran while one was open for 4% -> 4% of each run, Pallas kernels for 18% -> 20%
where the time goes in v1:
time: 153 us; the launch traced here: 152 us
  Pallas kernels  56.5 us (37%)
  waiting for transfers between devices  45.5 us (30%)
  starting transfers between devices  23.4 us (15%)
  between operations  13.5 us (9%)
  local copies, waits for them, and re-layouts  12.6 us (8%)
    ppermute x4, waiting for transfers between devices, hop(): lax.ppermute(sides[0], 'grp', right)  40.8 us
    pallas_call x1, Pallas kernels, finish(): pl.pallas_call(finish_kernel, out_shape=jax.ShapeDtypeStruct((species, pa...  26.1 us
    pallas_call x1, Pallas kernels, mix(): pl.pallas_call(functools.partial(mix_kernel, first, size, len(parts)), ou...  11.2 us
    ppermute x4, starting transfers between devices, hop(): lax.ppermute(sides[1], 'grp', left)  10.8 us
    pallas_call x1, Pallas kernels, unpack(): pl.pallas_call(unpack_kernel, out_shape=(jax.ShapeDtypeStruct((count, spe...  10 us
    all_to_all x1, starting transfers between devices, shards(): lax.all_to_all(packed, 'band', split_axis=0, concat_axis=0, tiled=True)  8.46 us
    pallas_call x1, Pallas kernels, pack(): pl.pallas_call(pack_kernel, out_shape=jax.ShapeDtypeStruct((count, rows,...  5.48 us
    unnamed x25, local copies, waits for them, and re-layouts  5.42 us
  transfers between devices with their start and end apart: 10, of which 5 were waited for; matrix products, arithmetic and copies ran while one was open for 4% of the time, Pallas kernels for 20%

profile of v1, /device:TPU:1, one launch (start us, length us, event | category | flops | bytes accessed | tf_op | source)
XLA Modules:
  0.0 152.2 jit_solution(511533031719471353)
XLA Ops:
  6.5 2.5 %slice.20 = bf16[112,4096]{1,0:T(8,128)(2,1)} slice(f32[160,4096]{1,0:T(8,128)} %bitcast.7), slice={[0:112], [0:4096]} | slice | bytes 1835008 | tf_op jit(solution)/shard_map/slice | solution.py:485
  9.1 1.2 slice.17.refs_5_
  10.3 2.5 %collective-permute-start = (bf16[48,4096]{1,0:T(8,128)(2,1)S(1)}, bf16[48,4096]{1,0:T(8,128)(2,1)S(1)}, u32[]{:S(2)}, u32[]{:S(2)}) collective-permute-start(bf16[48,4096]{1,0:T(8,128)(2,1)S(1)} %slice.17.refs_5_), channel_id=1, source_target_pairs={{0,1},{1,2},{2,3},{3,4},{4,5},{5,6},{6,7},{7,0},{8,9},{9,10},{10,1... | collective-permute-start | bytes 1179656 | tf_op jit(solution)/shard_map/ppermute | solution.py:450
  12.8 4.0 %collective-permute-start.1 = (bf16[48,4096]{1,0:T(8,128)(2,1)S(1)}, bf16[48,4096]{1,0:T(8,128)(2,1)S(1)}, u32[]{:S(2)}, u32[]{:S(2)}) collective-permute-start(bf16[48,4096]{1,0:T(8,128)(2,1)S(1)} %slice.17.refs_5_), channel_id=1, source_target_pairs={{0,7},{1,0},{2,1},{3,2},{4,3},{5,4},{6,5},{7,6},{8,15},{9,8},{10,9... | collective-permute-start | bytes 1179656 | tf_op jit(solution)/shard_map/ppermute | solution.py:450
  16.8 8.8 %collective-permute-done.refs_6_ = bf16[48,4096]{1,0:T(8,128)(2,1)S(1)} collective-permute-done((bf16[48,4096]{1,0:T(8,128)(2,1)S(1)}, bf16[48,4096]{1,0:T(8,128)(2,1)S(1)}, u32[]{:S(2)}, u32[]{:S(2)}) %collective-permute-start) | collective-permute-done | bytes 393248 | tf_op jit(solution)/shard_map/ppermute | solution.py:450
  25.6 0.8 copy-done.3
  26.4 0.8 copy-done.4
  27.1 5.5 %shard_map.91 = f32[32,208,128]{2,1,0:T(8,128)} custom-call(f32[32,160,160]{2,1,0:T(8,128)} %tiles_ref, s32[32,128]{1,0:T(8,128)} %bitcast.14), custom_call_target="tpu_custom_call" | custom-call | flops 1 | bytes 1 | tf_op jit(solution)/shard_map/pallas_call | solution.py:59
  32.6 8.5 %all-to-all-start = ((f32[32,208,128]{2,1,0:T(8,128)}), f32[32,208,128]{2,1,0:T(8,128)S(1)}, u32[]{:S(2)}, u32[]{:S(2)}) async-start(f32[32,208,128]{2,1,0:T(8,128)} %shard_map.91), calls=%async_computation | async-start | bytes 6815744 | tf_op jit(solution)/shard_map/all_to_all | solution.py:495
  41.2 2.8 %collective-permute-start.3 = (bf16[48,4096]{1,0:T(8,128)(2,1)}, bf16[48,4096]{1,0:T(8,128)(2,1)}, u32[]{:S(2)}, u32[]{:S(2)}) collective-permute-start(bf16[48,4096]{1,0:T(8,128)(2,1)} %copy-done.4), channel_id=1, source_target_pairs={{0,7},{1,0},{2,1},{3,2},{4,3},{5,4},{6,5},{7,6},{8,15},{9,8},{10,9... | collective-permute-start | bytes 1179656 | tf_op jit(solution)/shard_map/ppermute | solution.py:450
  43.9 3.8 %shard_map.92.refs_4_.select_ref = bf16[4096,256]{1,0:T(8,128)(2,1)} custom-call(s32[1,4096]{1,0:T(1,128)} %slots_ref.3), custom_call_target="tpu_custom_call" | custom-call | flops 1 | bytes 1 | tf_op jit(solution)/shard_map/pallas_call | solution.py:143
  47.7 14.3 %collective-permute-done.2.refs_7_ = bf16[48,4096]{1,0:T(8,128)(2,1)S(1)} collective-permute-done((bf16[48,4096]{1,0:T(8,128)(2,1)}, bf16[48,4096]{1,0:T(8,128)(2,1)S(1)}, u32[]{:S(2)}, u32[]{:S(2)}) %collective-permute-start.2) | collective-permute-done | bytes 393248 | tf_op jit(solution)/shard_map/ppermute | solution.py:450
  62.0 1.4 collective-permute-start.4
  63.4 1.3 collective-permute-start.5
  64.7 17.7 %collective-permute-done.4.refs_8_ = bf16[48,4096]{1,0:T(8,128)(2,1)S(1)} collective-permute-done((bf16[48,4096]{1,0:T(8,128)(2,1)S(1)}, bf16[48,4096]{1,0:T(8,128)(2,1)S(1)}, u32[]{:S(2)}, u32[]{:S(2)}) %collective-permute-start.4) | collective-permute-done | bytes 393248 | tf_op jit(solution)/shard_map/ppermute | solution.py:450
  82.4 0.8 copy-done.2
  83.7 1.8 %slice.16 = bf16[32,4096]{1,0:T(8,128)(2,1)} slice(bf16[48,4096]{1,0:T(8,128)(2,1)} %collective-permute-done.5.refs_9_), slice={[16:48], [0:4096]} | slice | bytes 524288 | tf_op jit(solution)/shard_map/slice | solution.py:459
  85.6 2.7 %collective-permute-start.7 = (bf16[32,4096]{1,0:T(8,128)(2,1)}, bf16[32,4096]{1,0:T(8,128)(2,1)}, u32[]{:S(2)}, u32[]{:S(2)}) collective-permute-start(bf16[32,4096]{1,0:T(8,128)(2,1)} %slice.16), channel_id=1, source_target_pairs={{0,7},{1,0},{2,1},{3,2},{4,3},{5,4},{6,5},{7,6},{8,15},{9,8},{10,9... | collective-permute-start | bytes 786440 | tf_op jit(solution)/shard_map/ppermute | solution.py:450
  89.1 1.7 %copy.17 = f32[160,160]{0,1:T(8,128)} copy(f32[160,160]{1,0:T(8,128)} %param.15) | data formatting | bytes 204800 | tf_op args[6]
  91.5 0.9 slice.15
  93.2 10.0 %shard_map.93 = (bf16[32,160,480]{2,1,0:T(8,128)(2,1)}, f32[160,4096]{1,0:T(8,128)}) custom-call(f32[32,208,128]{2,1,0:T(8,128)} %copy-done, f32[160,64]{1,0:T(8,128)} %bitcast.13), custom_call_target="tpu_custom_call" | custom-call | flops 1 | bytes 1 | tf_op jit(solution)/shard_map/pallas_call | solution.py:108
  103.8 11.2 %shard_map.94 = (f32[48,4096]{1,0:T(8,128)}, f32[48,4096]{1,0:T(8,128)}) custom-call(s32[32,3]{1,0:T(8,128)} %fusion.3.refs_0_, s32[1,4096]{1,0:T(1,128)} %slots_ref.3, bf16[32,3,128,128]{3,2,1,0:T(8,128)(2,1)} %weights_ref.1, f32[160,4096]{1,0:T(8,128)} %bitcast.9, bf16[4096,256]{1,0:T(8,128)(2,1)} %shard_map.92.refs_4_.select_ref, ...), custom_call_target="tpu_custom_call" | custom-call | flops 1 | bytes 1 | tf_op jit(solution)/shard_map/pallas_call | solution.py:226
  115.0 4.2 %all-gather.3.cloned.1.call-done = bf16[896,4096]{1,0:T(8,128)(2,1)} async-done(((bf16[112,4096]{1,0:T(8,128)(2,1)}), bf16[896,4096]{1,0:T(8,128)(2,1)}) %all-gather.3.cloned.1.call-update) | async-done | bytes 7340048 | tf_op jit(solution)/shard_map/all_gather | solution.py:489
  119.2 26.1 %shard_map.95 = f32[160,4096]{1,0:T(8,128)} custom-call(s32[32,3]{1,0:T(8,128)} %copy-done.6, s32[1,4096]{1,0:T(1,128)} %slots_ref.3, f32[160,160]{1,0:T(8,128)} %bitcast.12, f32[160,1]{1,0:T(8,128)} %copy.24.loss_ref, bf16[8,112,4096]{2,1,0:T(8,128)(2,1)} %bitcast.11, bf16[32,3,128,128]{3,2,1,0:T(8,128)(2,1)} %weights_ref.1, f32[160,4096]{1,0:T(8,128)} %bitcast.10, ...), custom_call_target="tpu_custom_call" | custom-call | flops 1 | bytes 1 | tf_op jit(solution)/shard_map/pallas_call | solution.py:415
  (33 shorter events, 3.6 us)
Async XLA Ops:
  6.5 112.7 %all-gather.3.cloned.1.call-start = ((), (), s32[]{:S(2)}) async-start(), calls=%async_computation.1 | async-start | bytes 8257536 | tf_op jit(solution)/shard_map/all_gather | solution.py:489
  10.2 22.4 %copy-start.1 = (bf16[48,4096]{1,0:T(8,128)(2,1)}, bf16[48,4096]{1,0:T(8,128)(2,1)S(1)}, u32[]{:S(2)}) copy-start(bf16[48,4096]{1,0:T(8,128)(2,1)S(1)} %slice.17.refs_5_) | copy-start | bytes 1179652
  10.3 15.3 %collective-permute-start = (bf16[48,4096]{1,0:T(8,128)(2,1)S(1)}, bf16[48,4096]{1,0:T(8,128)(2,1)S(1)}, u32[]{:S(2)}, u32[]{:S(2)}) collective-permute-start(bf16[48,4096]{1,0:T(8,128)(2,1)S(1)} %slice.17.refs_5_), channel_id=1, source_target_pairs={{0,1},{1,2},{2,3},{3,4},{4,5},{5,6},{6,7},{7,0},{8,9},{9,10},{10,1... | collective-permute-start | bytes 1179656 | tf_op jit(solution)/shard_map/ppermute | solution.py:450
  12.8 12.8 %collective-permute-start.1 = (bf16[48,4096]{1,0:T(8,128)(2,1)S(1)}, bf16[48,4096]{1,0:T(8,128)(2,1)S(1)}, u32[]{:S(2)}, u32[]{:S(2)}) collective-permute-start(bf16[48,4096]{1,0:T(8,128)(2,1)S(1)} %slice.17.refs_5_), channel_id=1, source_target_pairs={{0,7},{1,0},{2,1},{3,2},{4,3},{5,4},{6,5},{7,6},{8,15},{9,8},{10,9... | collective-permute-start | bytes 1179656 | tf_op jit(solution)/shard_map/ppermute | solution.py:450
  25.6 0.8 copy-start.3
  26.4 0.8 copy-start.4
  32.6 55.7 %copy-start.9 = (s32[32,3]{0,1:T(4,128)S(1)}, s32[32,3]{0,1:T(4,128)}, u32[]{:S(2)}) copy-start(s32[32,3]{0,1:T(4,128)} %param.10) | copy-start | bytes 1156
  32.6 55.8 %copy-start.8 = (f32[64,160]{1,0:T(8,128)S(1)}, f32[64,160]{1,0:T(8,128)}, u32[]{:S(2)}) copy-start(f32[64,160]{1,0:T(8,128)} %param.14) | copy-start | bytes 122884
  32.6 58.2 %copy-start.10 = (f32[160]{0:T(256)S(1)}, f32[160]{0:T(256)}, u32[]{:S(2)}) copy-start(f32[160]{0:T(256)} %param.16) | copy-start | bytes 1924
  32.6 51.1 %all-to-all-start = ((f32[32,208,128]{2,1,0:T(8,128)}), f32[32,208,128]{2,1,0:T(8,128)S(1)}, u32[]{:S(2)}, u32[]{:S(2)}) async-start(f32[32,208,128]{2,1,0:T(8,128)} %shard_map.91), calls=%async_computation | async-start | bytes 6815744 | tf_op jit(solution)/shard_map/all_to_all | solution.py:495
  41.1 20.9 %collective-permute-start.2 = (bf16[48,4096]{1,0:T(8,128)(2,1)}, bf16[48,4096]{1,0:T(8,128)(2,1)S(1)}, u32[]{:S(2)}, u32[]{:S(2)}) collective-permute-start(bf16[48,4096]{1,0:T(8,128)(2,1)} %copy-done.3), channel_id=1, source_target_pairs={{0,1},{1,2},{2,3},{3,4},{4,5},{5,6},{6,7},{7,0},{8,9},{9,10},{10,1... | collective-permute-start | bytes 1179656 | tf_op jit(solution)/shard_map/ppermute | solution.py:450
  41.2 20.9 %collective-permute-start.3 = (bf16[48,4096]{1,0:T(8,128)(2,1)}, bf16[48,4096]{1,0:T(8,128)(2,1)}, u32[]{:S(2)}, u32[]{:S(2)}) collective-permute-start(bf16[48,4096]{1,0:T(8,128)(2,1)} %copy-done.4), channel_id=1, source_target_pairs={{0,7},{1,0},{2,1},{3,2},{4,3},{5,4},{6,5},{7,6},{8,15},{9,8},{10,9... | collective-permute-start | bytes 1179656 | tf_op jit(solution)/shard_map/ppermute | solution.py:450
  62.0 20.4 %copy-start.5 = (bf16[48,4096]{1,0:T(8,128)(2,1)}, bf16[48,4096]{1,0:T(8,128)(2,1)S(1)}, u32[]{:S(2)}) copy-start(bf16[48,4096]{1,0:T(8,128)(2,1)S(1)} %collective-permute-done.2.refs_7_) | copy-start | bytes 1179652
  62.0 20.4 %collective-permute-start.4 = (bf16[48,4096]{1,0:T(8,128)(2,1)S(1)}, bf16[48,4096]{1,0:T(8,128)(2,1)S(1)}, u32[]{:S(2)}, u32[]{:S(2)}) collective-permute-start(bf16[48,4096]{1,0:T(8,128)(2,1)S(1)} %collective-permute-done.2.refs_7_), channel_id=1, source_target_pairs={{0,1},{1,2},{2,3},{3,4},{4,5},{5,6},{6,7},{7,0},{8,9},{9,10},{10,1... | collective-permute-start | bytes 1179656 | tf_op jit(solution)/shard_map/ppermute | solution.py:450
  63.4 19.8 %collective-permute-start.5 = (bf16[48,4096]{1,0:T(8,128)(2,1)}, bf16[48,4096]{1,0:T(8,128)(2,1)}, u32[]{:S(2)}, u32[]{:S(2)}) collective-permute-start(bf16[48,4096]{1,0:T(8,128)(2,1)} %collective-permute-done.3.refs_10_), channel_id=1, source_target_pairs={{0,7},{1,0},{2,1},{3,2},{4,3},{5,4},{6,5},{7,6},{8,15},{9,8},{10,9... | collective-permute-start | bytes 1179656 | tf_op jit(solution)/shard_map/ppermute | solution.py:450
  82.4 0.8 copy-start.2
  83.7 9.4 %copy-start = (f32[32,208,128]{2,1,0:T(8,128)}, f32[32,208,128]{2,1,0:T(8,128)S(1)}, u32[]{:S(2)}) copy-start(f32[32,208,128]{2,1,0:T(8,128)S(1)} %all-to-all-done.packed_ref) | copy-start | bytes 10223620
  85.6 17.6 %collective-permute-start.7 = (bf16[32,4096]{1,0:T(8,128)(2,1)}, bf16[32,4096]{1,0:T(8,128)(2,1)}, u32[]{:S(2)}, u32[]{:S(2)}) collective-permute-start(bf16[32,4096]{1,0:T(8,128)(2,1)} %slice.16), channel_id=1, source_target_pairs={{0,7},{1,0},{2,1},{3,2},{4,3},{5,4},{6,5},{7,6},{8,15},{9,8},{10,9... | collective-permute-start | bytes 786440 | tf_op jit(solution)/shard_map/ppermute | solution.py:450
  88.4 26.7 %copy-start.6 = (s32[32,3]{1,0:T(8,128)}, s32[32,3]{1,0:T(8,128)S(1)}, u32[]{:S(2)}) copy-start(s32[32,3]{1,0:T(8,128)S(1)} %copy.23.near_ref) | copy-start | bytes 1156
  92.4 10.8 %collective-permute-start.6 = (bf16[16,4096]{1,0:T(8,128)(2,1)S(1)}, bf16[16,4096]{1,0:T(8,128)(2,1)S(1)}, u32[]{:S(2)}, u32[]{:S(2)}) collective-permute-start(bf16[16,4096]{1,0:T(8,128)(2,1)S(1)} %slice.15), channel_id=1, source_target_pairs={{0,1},{1,2},{2,3},{3,4},{4,5},{5,6},{6,7},{7,0},{8,9},{9,10},{10,1... | collective-permute-start | bytes 393224 | tf_op jit(solution)/shard_map/ppermute | solution.py:450
  103.2 0.6 copy-start.7
Sparse Core Ops, SparseCore 0:
  10.4 108.7 all-gather.2

commit v2 on v1

--- a/solution.py
+++ b/solution.py
@@ -17,6 +17,8 @@
 
 f32 = jnp.float32
 bf16 = jnp.bfloat16
+f8 = jnp.float8_e4m3fn
+LOW_SCALE = 128.0
 VMEM = pl.BlockSpec(memory_space=pltpu.VMEM)
 SMEM = pl.BlockSpec(memory_space=pltpu.SMEM)
 ANY = pl.BlockSpec(memory_space=pl.ANY)
@@ -249,7 +251,7 @@
     near_ref, slots_ref, yields_ref, loss_ref,
     gathered_ref, weights_ref, comp_ref, select_ref, mixed_ref, start_ref, rates_ref, tiles_ref,
     out_ref,
-    held, weights, chosen, home, both, stack, begun, rates_in, tiles, delta, result,
+    held, weights, chosen, fine, home, both, stack, stack_low, begun, rates_in, tiles, delta, result,
     sems, lot_sems, out_sems,
 ):
     species, parcels = rates_in.shape
@@ -318,7 +320,7 @@
         home[pl.ds(0, size), pl.ds(off, BLOCK)] = total
         high, low = halves(total)
         both[pl.ds(0, size), pl.ds(off, BLOCK)] = high
-        both[pl.ds(size, size), pl.ds(off, BLOCK)] = low
+        both[pl.ds(size, size), pl.ds(off, BLOCK)] = low * LOW_SCALE
         return 0
 
     for n in range(lots):
@@ -328,21 +330,27 @@
 
     group = slots_ref[...] >> 8
 
+    fine[...] = chosen[...].astype(f8)
+
     def lay(i):
+        lows = []
         for j in range(GROUPS):
             keep = (group == i * GROUPS + j).astype(f32).astype(bf16)
-            stack[i % 2, pl.ds(j * 2 * size, 2 * size), :] = both[...] * keep
+            stack[i % 2, pl.ds(j * size, size), :] = both[pl.ds(0, size), :] * keep
+            lows.append(both[pl.ds(size, size), :] * keep)
+        stack_low[i % 2] = jnp.concatenate(lows, axis=0).astype(f8)
 
     lay(0)
     for i in range(wide // GROUPS):
         if i + 1 < wide // GROUPS:
             lay(i + 1)
         moved = jnp.dot(stack[i % 2], chosen[...], preferred_element_type=f32)
+        moved_low = jnp.dot(stack_low[i % 2], fine[...], preferred_element_type=f32)
         for j in range(GROUPS):
-            at = j * 2 * size
             off = (i * GROUPS + j) * WIDE
             begun[pl.ds(0, size), pl.ds(off, WIDE)] = (
-                moved[at : at + size] + moved[at + size : at + 2 * size]
+                moved[j * size : (j + 1) * size]
+                + moved_low[j * size : (j + 1) * size] * (1 / LOW_SCALE)
             )
 
     start_copy.wait()
@@ -421,9 +429,11 @@
             pltpu.VMEM(gathered.shape, bf16),
             pltpu.VMEM(weights.shape, bf16),
             pltpu.VMEM(chosen.shape, bf16),
+            pltpu.VMEM(chosen.shape, f8),
             whole,
             pltpu.VMEM((2 * size, parcels), bf16),
-            pltpu.VMEM((2, GROUPS * 2 * size, parcels), bf16),
+            pltpu.VMEM((2, GROUPS * size, parcels), bf16),
+            pltpu.VMEM((2, GROUPS * size, parcels), f8),
             whole,
             whole,
             pltpu.VMEM(tiles.shape, bf16),

time: 153 us -> 151 us (0.987)
  Pallas kernels: 56.5 us -> 54.6 us
    pallas_call x1, Pallas kernels: 26.1 us -> 24.2 us  [finish(): pl.pallas_call(finish_kernel, out_shape=jax.ShapeDtypeStruct((species, pa...]
where the time goes in v2:
time: 151 us; the launch traced here: 150 us
  Pallas kernels  54.6 us (36%)
  waiting for transfers between devices  45.5 us (30%)
  starting transfers between devices  23.4 us (15%)
  between operations  13.5 us (9%)
  local copies, waits for them, and re-layouts  12.6 us (8%)
    ppermute x4, waiting for transfers between devices, hop(): lax.ppermute(sides[0], 'grp', right)  40.8 us
    pallas_call x1, Pallas kernels, finish(): pl.pallas_call(finish_kernel, out_shape=jax.ShapeDtypeStruct((species, pa...  24.2 us
    pallas_call x1, Pallas kernels, mix(): pl.pallas_call(functools.partial(mix_kernel, first, size, len(parts)), ou...  11.2 us
    ppermute x4, starting transfers between devices, hop(): lax.ppermute(sides[1], 'grp', left)  10.8 us
    pallas_call x1, Pallas kernels, unpack(): pl.pallas_call(unpack_kernel, out_shape=(jax.ShapeDtypeStruct((count, spe...  10 us
    all_to_all x1, starting transfers between devices, shards(): lax.all_to_all(packed, 'band', split_axis=0, concat_axis=0, tiled=True)  8.46 us
    pallas_call x1, Pallas kernels, pack(): pl.pallas_call(pack_kernel, out_shape=jax.ShapeDtypeStruct((count, rows,...  5.48 us
    unnamed x25, local copies, waits for them, and re-layouts  5.42 us
  transfers between devices with their start and end apart: 10, of which 5 were waited for; matrix products, arithmetic and copies ran while one was open for 4% of the time, Pallas kernels for 20%

profile of v2, /device:TPU:1, one launch (start us, length us, event | category | flops | bytes accessed | tf_op | source)
XLA Modules:
  0.0 150.3 jit_solution(3799703170824075398)
XLA Ops:
  6.5 2.5 %slice.20 = bf16[112,4096]{1,0:T(8,128)(2,1)} slice(f32[160,4096]{1,0:T(8,128)} %bitcast.7), slice={[0:112], [0:4096]} | slice | bytes 1835008 | tf_op jit(solution)/shard_map/slice | solution.py:495
  9.1 1.2 slice.17.refs_5_
  10.3 2.5 %collective-permute-start = (bf16[48,4096]{1,0:T(8,128)(2,1)S(1)}, bf16[48,4096]{1,0:T(8,128)(2,1)S(1)}, u32[]{:S(2)}, u32[]{:S(2)}) collective-permute-start(bf16[48,4096]{1,0:T(8,128)(2,1)S(1)} %slice.17.refs_5_), channel_id=1, source_target_pairs={{0,1},{1,2},{2,3},{3,4},{4,5},{5,6},{6,7},{7,0},{8,9},{9,10},{10,1... | collective-permute-start | bytes 1179656 | tf_op jit(solution)/shard_map/ppermute | solution.py:460
  12.8 4.0 %collective-permute-start.1 = (bf16[48,4096]{1,0:T(8,128)(2,1)S(1)}, bf16[48,4096]{1,0:T(8,128)(2,1)S(1)}, u32[]{:S(2)}, u32[]{:S(2)}) collective-permute-start(bf16[48,4096]{1,0:T(8,128)(2,1)S(1)} %slice.17.refs_5_), channel_id=1, source_target_pairs={{0,7},{1,0},{2,1},{3,2},{4,3},{5,4},{6,5},{7,6},{8,15},{9,8},{10,9... | collective-permute-start | bytes 1179656 | tf_op jit(solution)/shard_map/ppermute | solution.py:460
  16.8 8.8 %collective-permute-done.refs_6_ = bf16[48,4096]{1,0:T(8,128)(2,1)S(1)} collective-permute-done((bf16[48,4096]{1,0:T(8,128)(2,1)S(1)}, bf16[48,4096]{1,0:T(8,128)(2,1)S(1)}, u32[]{:S(2)}, u32[]{:S(2)}) %collective-permute-start) | collective-permute-done | bytes 393248 | tf_op jit(solution)/shard_map/ppermute | solution.py:460
  25.6 0.8 copy-done.3
  26.4 0.8 copy-done.4
  27.1 5.5 %shard_map.91 = f32[32,208,128]{2,1,0:T(8,128)} custom-call(f32[32,160,160]{2,1,0:T(8,128)} %tiles_ref, s32[32,128]{1,0:T(8,128)} %bitcast.14), custom_call_target="tpu_custom_call" | custom-call | flops 1 | bytes 1 | tf_op jit(solution)/shard_map/pallas_call | solution.py:61
  32.6 8.5 %all-to-all-start = ((f32[32,208,128]{2,1,0:T(8,128)}), f32[32,208,128]{2,1,0:T(8,128)S(1)}, u32[]{:S(2)}, u32[]{:S(2)}) async-start(f32[32,208,128]{2,1,0:T(8,128)} %shard_map.91), calls=%async_computation | async-start | bytes 6815744 | tf_op jit(solution)/shard_map/all_to_all | solution.py:505
  41.2 2.8 %collective-permute-start.3 = (bf16[48,4096]{1,0:T(8,128)(2,1)}, bf16[48,4096]{1,0:T(8,128)(2,1)}, u32[]{:S(2)}, u32[]{:S(2)}) collective-permute-start(bf16[48,4096]{1,0:T(8,128)(2,1)} %copy-done.4), channel_id=1, source_target_pairs={{0,7},{1,0},{2,1},{3,2},{4,3},{5,4},{6,5},{7,6},{8,15},{9,8},{10,9... | collective-permute-start | bytes 1179656 | tf_op jit(solution)/shard_map/ppermute | solution.py:460
  43.9 3.8 %shard_map.92.refs_4_.select_ref = bf16[4096,256]{1,0:T(8,128)(2,1)} custom-call(s32[1,4096]{1,0:T(1,128)} %slots_ref.3), custom_call_target="tpu_custom_call" | custom-call | flops 1 | bytes 1 | tf_op jit(solution)/shard_map/pallas_call | solution.py:145
  47.7 14.3 %collective-permute-done.2.refs_7_ = bf16[48,4096]{1,0:T(8,128)(2,1)S(1)} collective-permute-done((bf16[48,4096]{1,0:T(8,128)(2,1)}, bf16[48,4096]{1,0:T(8,128)(2,1)S(1)}, u32[]{:S(2)}, u32[]{:S(2)}) %collective-permute-start.2) | collective-permute-done | bytes 393248 | tf_op jit(solution)/shard_map/ppermute | solution.py:460
  62.0 1.4 collective-permute-start.4
  63.4 1.3 collective-permute-start.5
  64.7 17.7 %collective-permute-done.4.refs_8_ = bf16[48,4096]{1,0:T(8,128)(2,1)S(1)} collective-permute-done((bf16[48,4096]{1,0:T(8,128)(2,1)S(1)}, bf16[48,4096]{1,0:T(8,128)(2,1)S(1)}, u32[]{:S(2)}, u32[]{:S(2)}) %collective-permute-start.4) | collective-permute-done | bytes 393248 | tf_op jit(solution)/shard_map/ppermute | solution.py:460
  82.4 0.8 copy-done.2
  83.7 1.8 %slice.16 = bf16[32,4096]{1,0:T(8,128)(2,1)} slice(bf16[48,4096]{1,0:T(8,128)(2,1)} %collective-permute-done.5.refs_9_), slice={[16:48], [0:4096]} | slice | bytes 524288 | tf_op jit(solution)/shard_map/slice | solution.py:469
  85.6 2.7 %collective-permute-start.7 = (bf16[32,4096]{1,0:T(8,128)(2,1)}, bf16[32,4096]{1,0:T(8,128)(2,1)}, u32[]{:S(2)}, u32[]{:S(2)}) collective-permute-start(bf16[32,4096]{1,0:T(8,128)(2,1)} %slice.16), channel_id=1, source_target_pairs={{0,7},{1,0},{2,1},{3,2},{4,3},{5,4},{6,5},{7,6},{8,15},{9,8},{10,9... | collective-permute-start | bytes 786440 | tf_op jit(solution)/shard_map/ppermute | solution.py:460
  89.1 1.7 %copy.17 = f32[160,160]{0,1:T(8,128)} copy(f32[160,160]{1,0:T(8,128)} %param.15) | data formatting | bytes 204800 | tf_op args[6]
  91.5 0.9 slice.15
  93.2 10.0 %shard_map.93 = (bf16[32,160,480]{2,1,0:T(8,128)(2,1)}, f32[160,4096]{1,0:T(8,128)}) custom-call(f32[32,208,128]{2,1,0:T(8,128)} %copy-done, f32[160,64]{1,0:T(8,128)} %bitcast.13), custom_call_target="tpu_custom_call" | custom-call | flops 1 | bytes 1 | tf_op jit(solution)/shard_map/pallas_call | solution.py:110
  103.8 11.2 %shard_map.94 = (f32[48,4096]{1,0:T(8,128)}, f32[48,4096]{1,0:T(8,128)}) custom-call(s32[32,3]{1,0:T(8,128)} %fusion.3.refs_0_, s32[1,4096]{1,0:T(1,128)} %slots_ref.3, bf16[32,3,128,128]{3,2,1,0:T(8,128)(2,1)} %weights_ref.1, f32[160,4096]{1,0:T(8,128)} %bitcast.9, bf16[4096,256]{1,0:T(8,128)(2,1)} %shard_map.92.refs_4_.select_ref, ...), custom_call_target="tpu_custom_call" | custom-call | flops 1 | bytes 1 | tf_op jit(solution)/shard_map/pallas_call | solution.py:228
  115.0 4.2 %all-gather.3.cloned.1.call-done = bf16[896,4096]{1,0:T(8,128)(2,1)} async-done(((bf16[112,4096]{1,0:T(8,128)(2,1)}), bf16[896,4096]{1,0:T(8,128)(2,1)}) %all-gather.3.cloned.1.call-update) | async-done | bytes 7340048 | tf_op jit(solution)/shard_map/all_gather | solution.py:499
  119.2 24.2 %shard_map.95 = f32[160,4096]{1,0:T(8,128)} custom-call(s32[32,3]{1,0:T(8,128)} %copy-done.6, s32[1,4096]{1,0:T(1,128)} %slots_ref.3, f32[160,160]{1,0:T(8,128)} %bitcast.12, f32[160,1]{1,0:T(8,128)} %copy.24.loss_ref, bf16[8,112,4096]{2,1,0:T(8,128)(2,1)} %bitcast.11, bf16[32,3,128,128]{3,2,1,0:T(8,128)(2,1)} %weights_ref.1, f32[160,4096]{1,0:T(8,128)} %bitcast.10, ...), custom_call_target="tpu_custom_call" | custom-call | flops 1 | bytes 1 | tf_op jit(solution)/shard_map/pallas_call | solution.py:423
  (33 shorter events, 3.6 us)
Async XLA Ops:
  6.5 112.7 %all-gather.3.cloned.1.call-start = ((), (), s32[]{:S(2)}) async-start(), calls=%async_computation.1 | async-start | bytes 8257536 | tf_op jit(solution)/shard_map/all_gather | solution.py:499
  10.2 22.4 %copy-start.1 = (bf16[48,4096]{1,0:T(8,128)(2,1)}, bf16[48,4096]{1,0:T(8,128)(2,1)S(1)}, u32[]{:S(2)}) copy-start(bf16[48,4096]{1,0:T(8,128)(2,1)S(1)} %slice.17.refs_5_) | copy-start | bytes 1179652
  10.3 15.3 %collective-permute-start = (bf16[48,4096]{1,0:T(8,128)(2,1)S(1)}, bf16[48,4096]{1,0:T(8,128)(2,1)S(1)}, u32[]{:S(2)}, u32[]{:S(2)}) collective-permute-start(bf16[48,4096]{1,0:T(8,128)(2,1)S(1)} %slice.17.refs_5_), channel_id=1, source_target_pairs={{0,1},{1,2},{2,3},{3,4},{4,5},{5,6},{6,7},{7,0},{8,9},{9,10},{10,1... | collective-permute-start | bytes 1179656 | tf_op jit(solution)/shard_map/ppermute | solution.py:460
  12.8 12.8 %collective-permute-start.1 = (bf16[48,4096]{1,0:T(8,128)(2,1)S(1)}, bf16[48,4096]{1,0:T(8,128)(2,1)S(1)}, u32[]{:S(2)}, u32[]{:S(2)}) collective-permute-start(bf16[48,4096]{1,0:T(8,128)(2,1)S(1)} %slice.17.refs_5_), channel_id=1, source_target_pairs={{0,7},{1,0},{2,1},{3,2},{4,3},{5,4},{6,5},{7,6},{8,15},{9,8},{10,9... | collective-permute-start | bytes 1179656 | tf_op jit(solution)/shard_map/ppermute | solution.py:460
  25.6 0.8 copy-start.3
  26.4 0.8 copy-start.4
  32.6 55.7 %copy-start.9 = (s32[32,3]{0,1:T(4,128)S(1)}, s32[32,3]{0,1:T(4,128)}, u32[]{:S(2)}) copy-start(s32[32,3]{0,1:T(4,128)} %param.10) | copy-start | bytes 1156
  32.6 55.8 %copy-start.8 = (f32[64,160]{1,0:T(8,128)S(1)}, f32[64,160]{1,0:T(8,128)}, u32[]{:S(2)}) copy-start(f32[64,160]{1,0:T(8,128)} %param.14) | copy-start | bytes 122884
  32.6 58.2 %copy-start.10 = (f32[160]{0:T(256)S(1)}, f32[160]{0:T(256)}, u32[]{:S(2)}) copy-start(f32[160]{0:T(256)} %param.16) | copy-start | bytes 1924
  32.6 51.1 %all-to-all-start = ((f32[32,208,128]{2,1,0:T(8,128)}), f32[32,208,128]{2,1,0:T(8,128)S(1)}, u32[]{:S(2)}, u32[]{:S(2)}) async-start(f32[32,208,128]{2,1,0:T(8,128)} %shard_map.91), calls=%async_computation | async-start | bytes 6815744 | tf_op jit(solution)/shard_map/all_to_all | solution.py:505
  41.1 20.9 %collective-permute-start.2 = (bf16[48,4096]{1,0:T(8,128)(2,1)}, bf16[48,4096]{1,0:T(8,128)(2,1)S(1)}, u32[]{:S(2)}, u32[]{:S(2)}) collective-permute-start(bf16[48,4096]{1,0:T(8,128)(2,1)} %copy-done.3), channel_id=1, source_target_pairs={{0,1},{1,2},{2,3},{3,4},{4,5},{5,6},{6,7},{7,0},{8,9},{9,10},{10,1... | collective-permute-start | bytes 1179656 | tf_op jit(solution)/shard_map/ppermute | solution.py:460
  41.2 20.9 %collective-permute-start.3 = (bf16[48,4096]{1,0:T(8,128)(2,1)}, bf16[48,4096]{1,0:T(8,128)(2,1)}, u32[]{:S(2)}, u32[]{:S(2)}) collective-permute-start(bf16[48,4096]{1,0:T(8,128)(2,1)} %copy-done.4), channel_id=1, source_target_pairs={{0,7},{1,0},{2,1},{3,2},{4,3},{5,4},{6,5},{7,6},{8,15},{9,8},{10,9... | collective-permute-start | bytes 1179656 | tf_op jit(solution)/shard_map/ppermute | solution.py:460
  62.0 20.4 %copy-start.5 = (bf16[48,4096]{1,0:T(8,128)(2,1)}, bf16[48,4096]{1,0:T(8,128)(2,1)S(1)}, u32[]{:S(2)}) copy-start(bf16[48,4096]{1,0:T(8,128)(2,1)S(1)} %collective-permute-done.2.refs_7_) | copy-start | bytes 1179652
  62.0 20.4 %collective-permute-start.4 = (bf16[48,4096]{1,0:T(8,128)(2,1)S(1)}, bf16[48,4096]{1,0:T(8,128)(2,1)S(1)}, u32[]{:S(2)}, u32[]{:S(2)}) collective-permute-start(bf16[48,4096]{1,0:T(8,128)(2,1)S(1)} %collective-permute-done.2.refs_7_), channel_id=1, source_target_pairs={{0,1},{1,2},{2,3},{3,4},{4,5},{5,6},{6,7},{7,0},{8,9},{9,10},{10,1... | collective-permute-start | bytes 1179656 | tf_op jit(solution)/shard_map/ppermute | solution.py:460
  63.4 19.8 %collective-permute-start.5 = (bf16[48,4096]{1,0:T(8,128)(2,1)}, bf16[48,4096]{1,0:T(8,128)(2,1)}, u32[]{:S(2)}, u32[]{:S(2)}) collective-permute-start(bf16[48,4096]{1,0:T(8,128)(2,1)} %collective-permute-done.3.refs_10_), channel_id=1, source_target_pairs={{0,7},{1,0},{2,1},{3,2},{4,3},{5,4},{6,5},{7,6},{8,15},{9,8},{10,9... | collective-permute-start | bytes 1179656 | tf_op jit(solution)/shard_map/ppermute | solution.py:460
  82.4 0.8 copy-start.2
  83.7 9.4 %copy-start = (f32[32,208,128]{2,1,0:T(8,128)}, f32[32,208,128]{2,1,0:T(8,128)S(1)}, u32[]{:S(2)}) copy-start(f32[32,208,128]{2,1,0:T(8,128)S(1)} %all-to-all-done.packed_ref) | copy-start | bytes 10223620
  85.6 17.6 %collective-permute-start.7 = (bf16[32,4096]{1,0:T(8,128)(2,1)}, bf16[32,4096]{1,0:T(8,128)(2,1)}, u32[]{:S(2)}, u32[]{:S(2)}) collective-permute-start(bf16[32,4096]{1,0:T(8,128)(2,1)} %slice.16), channel_id=1, source_target_pairs={{0,7},{1,0},{2,1},{3,2},{4,3},{5,4},{6,5},{7,6},{8,15},{9,8},{10,9... | collective-permute-start | bytes 786440 | tf_op jit(solution)/shard_map/ppermute | solution.py:460
  88.4 26.7 %copy-start.6 = (s32[32,3]{1,0:T(8,128)}, s32[32,3]{1,0:T(8,128)S(1)}, u32[]{:S(2)}) copy-start(s32[32,3]{1,0:T(8,128)S(1)} %copy.23.near_ref) | copy-start | bytes 1156
  92.4 10.8 %collective-permute-start.6 = (bf16[16,4096]{1,0:T(8,128)(2,1)S(1)}, bf16[16,4096]{1,0:T(8,128)(2,1)S(1)}, u32[]{:S(2)}, u32[]{:S(2)}) collective-permute-start(bf16[16,4096]{1,0:T(8,128)(2,1)S(1)} %slice.15), channel_id=1, source_target_pairs={{0,1},{1,2},{2,3},{3,4},{4,5},{5,6},{6,7},{7,0},{8,9},{9,10},{10,1... | collective-permute-start | bytes 393224 | tf_op jit(solution)/shard_map/ppermute | solution.py:460
  103.2 0.6 copy-start.7
Sparse Core Ops, SparseCore 0:
  10.4 108.7 all-gather.2

commit v3 on v2

--- a/solution.py
+++ b/solution.py
@@ -11,7 +11,7 @@
 NEWTON = 2
 WIDE = 256
 LIMIT = 60
-GROUPS = 2
+GROUPS = 4
 LOT = 8
 time_step = 0.5
 
@@ -375,7 +375,9 @@
                 jnp.dot(yields, spread(current * rates), preferred_element_type=f32)
                 - loss * current * current
             )
-            defect = current - start - time_step * forcing
+            defect = -time_step * forcing
+            if newton_step > 0:
+                defect = current - start + defect
             wings = spread(defect)
             update = [
                 jnp.dot(

time: 151 us -> 151 us (level)
  no operation moved by 1% of the time
where the time goes in v3:
time: 151 us; the launch traced here: 150 us
  Pallas kernels  53.9 us (36%)
  waiting for transfers between devices  46.2 us (31%)
  starting transfers between devices  23.4 us (15%)
  between operations  13.5 us (9%)
  local copies, waits for them, and re-layouts  12.6 us (8%)
    ppermute x4, waiting for transfers between devices, hop(): lax.ppermute(sides[0], 'grp', right)  40.8 us
    pallas_call x1, Pallas kernels, finish(): pl.pallas_call(finish_kernel, out_shape=jax.ShapeDtypeStruct((species, pa...  24.1 us
    ppermute x4, starting transfers between devices, hop(): lax.ppermute(sides[1], 'grp', left)  10.8 us
    pallas_call x1, Pallas kernels, mix(): pl.pallas_call(functools.partial(mix_kernel, first, size, len(parts)), ou...  10.5 us
    pallas_call x1, Pallas kernels, unpack(): pl.pallas_call(unpack_kernel, out_shape=(jax.ShapeDtypeStruct((count, spe...  10 us
    all_to_all x1, starting transfers between devices, shards(): lax.all_to_all(packed, 'band', split_axis=0, concat_axis=0, tiled=True)  8.46 us
    pallas_call x1, Pallas kernels, pack(): pl.pallas_call(pack_kernel, out_shape=jax.ShapeDtypeStruct((count, rows,...  5.48 us
    unnamed x25, local copies, waits for them, and re-layouts  5.42 us
  transfers between devices with their start and end apart: 10, of which 5 were waited for; matrix products, arithmetic and copies ran while one was open for 4% of the time, Pallas kernels for 20%

profile of v3, /device:TPU:1, one launch (start us, length us, event | category | flops | bytes accessed | tf_op | source)
XLA Modules:
  0.0 150.2 jit_solution(1319964869647020728)
XLA Ops:
  6.5 2.5 %slice.20 = bf16[112,4096]{1,0:T(8,128)(2,1)} slice(f32[160,4096]{1,0:T(8,128)} %bitcast.7), slice={[0:112], [0:4096]} | slice | bytes 1835008 | tf_op jit(solution)/shard_map/slice | solution.py:497
  9.1 1.2 slice.17.refs_5_
  10.3 2.5 %collective-permute-start = (bf16[48,4096]{1,0:T(8,128)(2,1)S(1)}, bf16[48,4096]{1,0:T(8,128)(2,1)S(1)}, u32[]{:S(2)}, u32[]{:S(2)}) collective-permute-start(bf16[48,4096]{1,0:T(8,128)(2,1)S(1)} %slice.17.refs_5_), channel_id=1, source_target_pairs={{0,1},{1,2},{2,3},{3,4},{4,5},{5,6},{6,7},{7,0},{8,9},{9,10},{10,1... | collective-permute-start | bytes 1179656 | tf_op jit(solution)/shard_map/ppermute | solution.py:462
  12.8 4.0 %collective-permute-start.1 = (bf16[48,4096]{1,0:T(8,128)(2,1)S(1)}, bf16[48,4096]{1,0:T(8,128)(2,1)S(1)}, u32[]{:S(2)}, u32[]{:S(2)}) collective-permute-start(bf16[48,4096]{1,0:T(8,128)(2,1)S(1)} %slice.17.refs_5_), channel_id=1, source_target_pairs={{0,7},{1,0},{2,1},{3,2},{4,3},{5,4},{6,5},{7,6},{8,15},{9,8},{10,9... | collective-permute-start | bytes 1179656 | tf_op jit(solution)/shard_map/ppermute | solution.py:462
  16.8 8.8 %collective-permute-done.refs_6_ = bf16[48,4096]{1,0:T(8,128)(2,1)S(1)} collective-permute-done((bf16[48,4096]{1,0:T(8,128)(2,1)S(1)}, bf16[48,4096]{1,0:T(8,128)(2,1)S(1)}, u32[]{:S(2)}, u32[]{:S(2)}) %collective-permute-start) | collective-permute-done | bytes 393248 | tf_op jit(solution)/shard_map/ppermute | solution.py:462
  25.6 0.8 copy-done.3
  26.4 0.8 copy-done.4
  27.1 5.5 %shard_map.91 = f32[32,208,128]{2,1,0:T(8,128)} custom-call(f32[32,160,160]{2,1,0:T(8,128)} %tiles_ref, s32[32,128]{1,0:T(8,128)} %bitcast.14), custom_call_target="tpu_custom_call" | custom-call | flops 1 | bytes 1 | tf_op jit(solution)/shard_map/pallas_call | solution.py:61
  32.6 8.5 %all-to-all-start = ((f32[32,208,128]{2,1,0:T(8,128)}), f32[32,208,128]{2,1,0:T(8,128)S(1)}, u32[]{:S(2)}, u32[]{:S(2)}) async-start(f32[32,208,128]{2,1,0:T(8,128)} %shard_map.91), calls=%async_computation | async-start | bytes 6815744 | tf_op jit(solution)/shard_map/all_to_all | solution.py:507
  41.2 2.8 %collective-permute-start.3 = (bf16[48,4096]{1,0:T(8,128)(2,1)}, bf16[48,4096]{1,0:T(8,128)(2,1)}, u32[]{:S(2)}, u32[]{:S(2)}) collective-permute-start(bf16[48,4096]{1,0:T(8,128)(2,1)} %copy-done.4), channel_id=1, source_target_pairs={{0,7},{1,0},{2,1},{3,2},{4,3},{5,4},{6,5},{7,6},{8,15},{9,8},{10,9... | collective-permute-start | bytes 1179656 | tf_op jit(solution)/shard_map/ppermute | solution.py:462
  43.9 3.8 %shard_map.92.refs_4_.select_ref = bf16[4096,256]{1,0:T(8,128)(2,1)} custom-call(s32[1,4096]{1,0:T(1,128)} %slots_ref.3), custom_call_target="tpu_custom_call" | custom-call | flops 1 | bytes 1 | tf_op jit(solution)/shard_map/pallas_call | solution.py:145
  47.7 14.3 %collective-permute-done.2.refs_7_ = bf16[48,4096]{1,0:T(8,128)(2,1)S(1)} collective-permute-done((bf16[48,4096]{1,0:T(8,128)(2,1)}, bf16[48,4096]{1,0:T(8,128)(2,1)S(1)}, u32[]{:S(2)}, u32[]{:S(2)}) %collective-permute-start.2) | collective-permute-done | bytes 393248 | tf_op jit(solution)/shard_map/ppermute | solution.py:462
  62.0 1.4 collective-permute-start.4
  63.4 1.3 collective-permute-start.5
  64.7 17.7 %collective-permute-done.4.refs_8_ = bf16[48,4096]{1,0:T(8,128)(2,1)S(1)} collective-permute-done((bf16[48,4096]{1,0:T(8,128)(2,1)S(1)}, bf16[48,4096]{1,0:T(8,128)(2,1)S(1)}, u32[]{:S(2)}, u32[]{:S(2)}) %collective-permute-start.4) | collective-permute-done | bytes 393248 | tf_op jit(solution)/shard_map/ppermute | solution.py:462
  82.4 0.8 copy-done.2
  83.7 1.8 %slice.16 = bf16[32,4096]{1,0:T(8,128)(2,1)} slice(bf16[48,4096]{1,0:T(8,128)(2,1)} %collective-permute-done.5.refs_9_), slice={[16:48], [0:4096]} | slice | bytes 524288 | tf_op jit(solution)/shard_map/slice | solution.py:471
  85.6 2.7 %collective-permute-start.7 = (bf16[32,4096]{1,0:T(8,128)(2,1)}, bf16[32,4096]{1,0:T(8,128)(2,1)}, u32[]{:S(2)}, u32[]{:S(2)}) collective-permute-start(bf16[32,4096]{1,0:T(8,128)(2,1)} %slice.16), channel_id=1, source_target_pairs={{0,7},{1,0},{2,1},{3,2},{4,3},{5,4},{6,5},{7,6},{8,15},{9,8},{10,9... | collective-permute-start | bytes 786440 | tf_op jit(solution)/shard_map/ppermute | solution.py:462
  89.1 1.7 %copy.17 = f32[160,160]{0,1:T(8,128)} copy(f32[160,160]{1,0:T(8,128)} %param.15) | data formatting | bytes 204800 | tf_op args[6]
  91.5 0.9 slice.15
  93.2 10.0 %shard_map.93 = (bf16[32,160,480]{2,1,0:T(8,128)(2,1)}, f32[160,4096]{1,0:T(8,128)}) custom-call(f32[32,208,128]{2,1,0:T(8,128)} %copy-done, f32[160,64]{1,0:T(8,128)} %bitcast.13), custom_call_target="tpu_custom_call" | custom-call | flops 1 | bytes 1 | tf_op jit(solution)/shard_map/pallas_call | solution.py:110
  103.8 10.5 %shard_map.94 = (f32[48,4096]{1,0:T(8,128)}, f32[48,4096]{1,0:T(8,128)}) custom-call(s32[32,3]{1,0:T(8,128)} %fusion.3.refs_0_, s32[1,4096]{1,0:T(1,128)} %slots_ref.3, bf16[32,3,128,128]{3,2,1,0:T(8,128)(2,1)} %weights_ref.1, f32[160,4096]{1,0:T(8,128)} %bitcast.9, bf16[4096,256]{1,0:T(8,128)(2,1)} %shard_map.92.refs_4_.select_ref, ...), custom_call_target="tpu_custom_call" | custom-call | flops 1 | bytes 1 | tf_op jit(solution)/shard_map/pallas_call | solution.py:228
  114.3 4.9 %all-gather.3.cloned.1.call-done = bf16[896,4096]{1,0:T(8,128)(2,1)} async-done(((bf16[112,4096]{1,0:T(8,128)(2,1)}), bf16[896,4096]{1,0:T(8,128)(2,1)}) %all-gather.3.cloned.1.call-update) | async-done | bytes 7340048 | tf_op jit(solution)/shard_map/all_gather | solution.py:501
  119.2 24.1 %shard_map.95 = f32[160,4096]{1,0:T(8,128)} custom-call(s32[32,3]{1,0:T(8,128)} %copy-done.6, s32[1,4096]{1,0:T(1,128)} %slots_ref.3, f32[160,160]{1,0:T(8,128)} %bitcast.12, f32[160,1]{1,0:T(8,128)} %copy.24.loss_ref, bf16[8,112,4096]{2,1,0:T(8,128)(2,1)} %bitcast.11, bf16[32,3,128,128]{3,2,1,0:T(8,128)(2,1)} %weights_ref.1, f32[160,4096]{1,0:T(8,128)} %bitcast.10, ...), custom_call_target="tpu_custom_call" | custom-call | flops 1 | bytes 1 | tf_op jit(solution)/shard_map/pallas_call | solution.py:425
  (33 shorter events, 3.6 us)
Async XLA Ops:
  6.5 112.7 %all-gather.3.cloned.1.call-start = ((), (), s32[]{:S(2)}) async-start(), calls=%async_computation.1 | async-start | bytes 8257536 | tf_op jit(solution)/shard_map/all_gather | solution.py:501
  10.2 22.4 %copy-start.1 = (bf16[48,4096]{1,0:T(8,128)(2,1)}, bf16[48,4096]{1,0:T(8,128)(2,1)S(1)}, u32[]{:S(2)}) copy-start(bf16[48,4096]{1,0:T(8,128)(2,1)S(1)} %slice.17.refs_5_) | copy-start | bytes 1179652
  10.3 15.3 %collective-permute-start = (bf16[48,4096]{1,0:T(8,128)(2,1)S(1)}, bf16[48,4096]{1,0:T(8,128)(2,1)S(1)}, u32[]{:S(2)}, u32[]{:S(2)}) collective-permute-start(bf16[48,4096]{1,0:T(8,128)(2,1)S(1)} %slice.17.refs_5_), channel_id=1, source_target_pairs={{0,1},{1,2},{2,3},{3,4},{4,5},{5,6},{6,7},{7,0},{8,9},{9,10},{10,1... | collective-permute-start | bytes 1179656 | tf_op jit(solution)/shard_map/ppermute | solution.py:462
  12.8 12.8 %collective-permute-start.1 = (bf16[48,4096]{1,0:T(8,128)(2,1)S(1)}, bf16[48,4096]{1,0:T(8,128)(2,1)S(1)}, u32[]{:S(2)}, u32[]{:S(2)}) collective-permute-start(bf16[48,4096]{1,0:T(8,128)(2,1)S(1)} %slice.17.refs_5_), channel_id=1, source_target_pairs={{0,7},{1,0},{2,1},{3,2},{4,3},{5,4},{6,5},{7,6},{8,15},{9,8},{10,9... | collective-permute-start | bytes 1179656 | tf_op jit(solution)/shard_map/ppermute | solution.py:462
  25.6 0.8 copy-start.3
  26.4 0.8 copy-start.4
  32.6 55.7 %copy-start.9 = (s32[32,3]{0,1:T(4,128)S(1)}, s32[32,3]{0,1:T(4,128)}, u32[]{:S(2)}) copy-start(s32[32,3]{0,1:T(4,128)} %param.10) | copy-start | bytes 1156
  32.6 55.8 %copy-start.8 = (f32[64,160]{1,0:T(8,128)S(1)}, f32[64,160]{1,0:T(8,128)}, u32[]{:S(2)}) copy-start(f32[64,160]{1,0:T(8,128)} %param.14) | copy-start | bytes 122884
  32.6 58.2 %copy-start.10 = (f32[160]{0:T(256)S(1)}, f32[160]{0:T(256)}, u32[]{:S(2)}) copy-start(f32[160]{0:T(256)} %param.16) | copy-start | bytes 1924
  32.6 51.1 %all-to-all-start = ((f32[32,208,128]{2,1,0:T(8,128)}), f32[32,208,128]{2,1,0:T(8,128)S(1)}, u32[]{:S(2)}, u32[]{:S(2)}) async-start(f32[32,208,128]{2,1,0:T(8,128)} %shard_map.91), calls=%async_computation | async-start | bytes 6815744 | tf_op jit(solution)/shard_map/all_to_all | solution.py:507
  41.1 20.9 %collective-permute-start.2 = (bf16[48,4096]{1,0:T(8,128)(2,1)}, bf16[48,4096]{1,0:T(8,128)(2,1)S(1)}, u32[]{:S(2)}, u32[]{:S(2)}) collective-permute-start(bf16[48,4096]{1,0:T(8,128)(2,1)} %copy-done.3), channel_id=1, source_target_pairs={{0,1},{1,2},{2,3},{3,4},{4,5},{5,6},{6,7},{7,0},{8,9},{9,10},{10,1... | collective-permute-start | bytes 1179656 | tf_op jit(solution)/shard_map/ppermute | solution.py:462
  41.2 20.9 %collective-permute-start.3 = (bf16[48,4096]{1,0:T(8,128)(2,1)}, bf16[48,4096]{1,0:T(8,128)(2,1)}, u32[]{:S(2)}, u32[]{:S(2)}) collective-permute-start(bf16[48,4096]{1,0:T(8,128)(2,1)} %copy-done.4), channel_id=1, source_target_pairs={{0,7},{1,0},{2,1},{3,2},{4,3},{5,4},{6,5},{7,6},{8,15},{9,8},{10,9... | collective-permute-start | bytes 1179656 | tf_op jit(solution)/shard_map/ppermute | solution.py:462
  62.0 20.4 %copy-start.5 = (bf16[48,4096]{1,0:T(8,128)(2,1)}, bf16[48,4096]{1,0:T(8,128)(2,1)S(1)}, u32[]{:S(2)}) copy-start(bf16[48,4096]{1,0:T(8,128)(2,1)S(1)} %collective-permute-done.2.refs_7_) | copy-start | bytes 1179652
  62.0 20.4 %collective-permute-start.4 = (bf16[48,4096]{1,0:T(8,128)(2,1)S(1)}, bf16[48,4096]{1,0:T(8,128)(2,1)S(1)}, u32[]{:S(2)}, u32[]{:S(2)}) collective-permute-start(bf16[48,4096]{1,0:T(8,128)(2,1)S(1)} %collective-permute-done.2.refs_7_), channel_id=1, source_target_pairs={{0,1},{1,2},{2,3},{3,4},{4,5},{5,6},{6,7},{7,0},{8,9},{9,10},{10,1... | collective-permute-start | bytes 1179656 | tf_op jit(solution)/shard_map/ppermute | solution.py:462
  63.4 19.8 %collective-permute-start.5 = (bf16[48,4096]{1,0:T(8,128)(2,1)}, bf16[48,4096]{1,0:T(8,128)(2,1)}, u32[]{:S(2)}, u32[]{:S(2)}) collective-permute-start(bf16[48,4096]{1,0:T(8,128)(2,1)} %collective-permute-done.3.refs_10_), channel_id=1, source_target_pairs={{0,7},{1,0},{2,1},{3,2},{4,3},{5,4},{6,5},{7,6},{8,15},{9,8},{10,9... | collective-permute-start | bytes 1179656 | tf_op jit(solution)/shard_map/ppermute | solution.py:462
  82.4 0.8 copy-start.2
  83.7 9.4 %copy-start = (f32[32,208,128]{2,1,0:T(8,128)}, f32[32,208,128]{2,1,0:T(8,128)S(1)}, u32[]{:S(2)}) copy-start(f32[32,208,128]{2,1,0:T(8,128)S(1)} %all-to-all-done.packed_ref) | copy-start | bytes 10223620
  85.6 17.6 %collective-permute-start.7 = (bf16[32,4096]{1,0:T(8,128)(2,1)}, bf16[32,4096]{1,0:T(8,128)(2,1)}, u32[]{:S(2)}, u32[]{:S(2)}) collective-permute-start(bf16[32,4096]{1,0:T(8,128)(2,1)} %slice.16), channel_id=1, source_target_pairs={{0,7},{1,0},{2,1},{3,2},{4,3},{5,4},{6,5},{7,6},{8,15},{9,8},{10,9... | collective-permute-start | bytes 786440 | tf_op jit(solution)/shard_map/ppermute | solution.py:462
  88.4 26.0 %copy-start.6 = (s32[32,3]{1,0:T(8,128)}, s32[32,3]{1,0:T(8,128)S(1)}, u32[]{:S(2)}) copy-start(s32[32,3]{1,0:T(8,128)S(1)} %copy.23.near_ref) | copy-start | bytes 1156
  92.4 10.8 %collective-permute-start.6 = (bf16[16,4096]{1,0:T(8,128)(2,1)S(1)}, bf16[16,4096]{1,0:T(8,128)(2,1)S(1)}, u32[]{:S(2)}, u32[]{:S(2)}) collective-permute-start(bf16[16,4096]{1,0:T(8,128)(2,1)S(1)} %slice.15), channel_id=1, source_target_pairs={{0,1},{1,2},{2,3},{3,4},{4,5},{5,6},{6,7},{7,0},{8,9},{9,10},{10,1... | collective-permute-start | bytes 393224 | tf_op jit(solution)/shard_map/ppermute | solution.py:462
  103.2 0.6 copy-start.7
Sparse Core Ops, SparseCore 0:
  10.4 108.7 all-gather.2
